TPU v7x, 32 devices: a whole 2x2x4 slice. The times are simulated.
32 devices in a mesh: dp: 16 (over z, x, core), tensor: 2 (over y).
Axes of the slice: x: 2, y: 2, z: 4, core: 2. Of those that a mesh axis runs over, the one named last changes fastest.
Arguments:
- tokens: bfloat16 [24576, 768], P('dp'), may hold values from -6 to 6
- cotangent: bfloat16 [24576, 768], P('dp'), may hold values from -6 to 6
- segment_ids: int32 [16, 1536], P('dp'), may hold values from 0 to 1, never falling along the last dimension, each value on 1 to 1024 neighbouring positions
- timesteps: int32 [16, 2], P('dp'), may hold values from 0 to 1999
- qkv_weight: float32 [768, 3, 768], P('dp', None, 'tensor'), may hold values from -0.25 to 0.25
- out_weight: float32 [768, 768], P('tensor', 'dp'), may hold values from -0.625 to 0.625
- up_weight: float32 [768, 4, 768], P('dp', None, 'tensor'), may hold values from -0.21875 to 0.21875
- down_weight: float32 [4, 768, 768], P(None, 'tensor', 'dp'), may hold values from -0.109375 to 0.109375
- time_inner: float32 [128, 512], P('dp'), may hold values from -0.5 to 0.5
- time_outer: float32 [512, 768], P('dp'), may hold values from -0.25 to 0.25
- time_bias: float32 [512], P('dp'), may hold values from -3 to 3
- head_vectors: float32 [6, 2, 384], P(None, 'tensor', 'dp'), may hold values from -1 to 1
- layer_vectors: float32 [7, 768], P(None, 'dp'), may hold values from 0.5 to 6
- qkv_moment: float32 [768, 3, 768], P('dp', None, 'tensor'), may hold values from -0.001953125 to 0.001953125
- out_moment: float32 [768, 768], P('tensor', 'dp'), may hold values from -0.001953125 to 0.001953125
- up_moment: float32 [768, 4, 768], P('dp', None, 'tensor'), may hold values from -0.001953125 to 0.001953125
- down_moment: float32 [4, 768, 768], P(None, 'tensor', 'dp'), may hold values from -0.001953125 to 0.001953125
- inner_moment: float32 [128, 512], P('dp'), may hold values from -0.001953125 to 0.001953125
- outer_moment: float32 [512, 768], P('dp'), may hold values from -0.001953125 to 0.001953125
- bias_moment: float32 [512], P('dp'), may hold values from -0.001953125 to 0.001953125
- head_moment: float32 [6, 2, 384], P(None, 'tensor', 'dp'), may hold values from -0.001953125 to 0.001953125
- layer_moment: float32 [7, 768], P(None, 'dp'), may hold values from -0.001953125 to 0.001953125
- qkv_average: float32 [768, 3, 768], P('dp', None, 'tensor'), may hold values from -0.25 to 0.25
- out_average: float32 [768, 768], P('tensor', 'dp'), may hold values from -0.625 to 0.625
- up_average: float32 [768, 4, 768], P('dp', None, 'tensor'), may hold values from -0.21875 to 0.21875
- down_average: float32 [4, 768, 768], P(None, 'tensor', 'dp'), may hold values from -0.109375 to 0.109375
- inner_average: float32 [128, 512], P('dp'), may hold values from -0.5 to 0.5
- outer_average: float32 [512, 768], P('dp'), may hold values from -0.25 to 0.25
- bias_average: float32 [512], P('dp'), may hold values from -3 to 3
- head_average: float32 [6, 2, 384], P(None, 'tensor', 'dp'), may hold values from -1 to 1
- layer_average: float32 [7, 768], P(None, 'dp'), may hold values from 0.5 to 1.5
Outputs:
- output: bfloat16 [24576, 768], P('dp')
- input_grad: bfloat16 [24576, 768], P('dp')
- norm: float32 [], replicated
- qkv_master: float32 [768, 3, 768], P('dp', None, 'tensor')
- out_master: float32 [768, 768], P('tensor', 'dp')
- up_master: float32 [768, 4, 768], P('dp', None, 'tensor')
- down_master: float32 [4, 768, 768], P(None, 'tensor', 'dp')
- inner_master: float32 [128, 512], P('dp')
- outer_master: float32 [512, 768], P('dp')
- bias_master: float32 [512], P('dp')
- head_master: float32 [6, 2, 384], P(None, 'tensor', 'dp')
- layer_master: float32 [7, 768], P(None, 'dp')
- qkv_velocity: float32 [768, 3, 768], P('dp', None, 'tensor')
- out_velocity: float32 [768, 768], P('tensor', 'dp')
- up_velocity: float32 [768, 4, 768], P('dp', None, 'tensor')
- down_velocity: float32 [4, 768, 768], P(None, 'tensor', 'dp')
- inner_velocity: float32 [128, 512], P('dp')
- outer_velocity: float32 [512, 768], P('dp')
- bias_velocity: float32 [512], P('dp')
- head_velocity: float32 [6, 2, 384], P(None, 'tensor', 'dp')
- layer_velocity: float32 [7, 768], P(None, 'dp')
- qkv_smoothed: float32 [768, 3, 768], P('dp', None, 'tensor')
- out_smoothed: float32 [768, 768], P('tensor', 'dp')
- up_smoothed: float32 [768, 4, 768], P('dp', None, 'tensor')
- down_smoothed: float32 [4, 768, 768], P(None, 'tensor', 'dp')
- inner_smoothed: float32 [128, 512], P('dp')
- outer_smoothed: float32 [512, 768], P('dp')
- bias_smoothed: float32 [512], P('dp')
- head_smoothed: float32 [6, 2, 384], P(None, 'tensor', 'dp')
- layer_smoothed: float32 [7, 768], P(None, 'dp')
Inputs may be any that keep to these rules, and one draw needn't show every extreme that they name: `segment_ids`: within each pack the sequence number never falls, and each of the 2 sequences holds 512 to 1024 tokens.
All inputs are finite; a program needn't handle non-finite values.
Results may differ from a plain program's by a relative error of at most 0.024.
The roundings to bfloat16 on the way count: a program that leaves them out, or rounds other values in their place, can miss the bound.
Values may be sent and summed in bfloat16 or wider, within the bound.
A program may use at most 128 MiB of HBM per device.

v0:
```python
import math

import jax
import jax.numpy as jnp
from jax import lax
from jax.sharding import PartitionSpec as P

D = 768
HD = 64
TD = 128
SEGS = 2
PACK = 1536
MPARAMS = 7536640


EPSILON = 1e-05
MOMENTUM = 0.5
AVERAGE_DECAY = 0.5


def layer_norm(values, gain_vec, shift_vec):
    centre = jnp.mean(values, axis=-1, keepdims=True)
    centred = values - centre
    spread = jnp.mean(centred * centred, axis=-1, keepdims=True)
    return centred * lax.rsqrt(spread + EPSILON) * gain_vec + shift_vec


def time_features(step_ids, feat_width):
    midpoint = feat_width // 2
    frequency = jnp.exp(-math.log(10000.0) * jnp.arange(midpoint, dtype=jnp.float32) / midpoint)
    angles = step_ids.astype(jnp.float32)[..., None] * frequency
    return jnp.concatenate([jnp.cos(angles), jnp.sin(angles)], axis=-1)


def gelu_exact(values):
    return jax.nn.gelu(values, approximate=False)


def head_slice(matrix, head_index):
    return lax.dynamic_slice_in_dim(matrix, head_index * HD, HD, 1)


def merge_heads(stacked):
    return stacked.transpose(1, 0, 2).reshape(stacked.shape[1], stacked.shape[0] * stacked.shape[2])


def advance(master, moment, average, grad, factor, step_rate):
    scaled = grad * factor
    velocity = MOMENTUM * moment + scaled
    fresh_master = master - step_rate * (scaled + MOMENTUM * velocity)
    smoothed = AVERAGE_DECAY * average + (1.0 - AVERAGE_DECAY) * fresh_master
    return (fresh_master, velocity, smoothed)


def shards(
    tokens,
    cotangent,
    segment_ids,
    timesteps,
    qkv_weight,
    out_weight,
    up_weight,
    down_weight,
    time_inner,
    time_outer,
    time_bias,
    head_vectors,
    layer_vectors,
    qkv_moment,
    out_moment,
    up_moment,
    down_moment,
    inner_moment,
    outer_moment,
    bias_moment,
    head_moment,
    layer_moment,
    qkv_average,
    out_average,
    up_average,
    down_average,
    inner_average,
    outer_average,
    bias_average,
    head_average,
    layer_average,
):
    w_qkv, w_out, w_up, w_down, w_inner, w_outer, b_inner, head_vec, layer_vec = (
        lax.all_gather(qkv_weight.astype(jnp.bfloat16), "dp", axis=0, tiled=True),
        lax.all_gather(out_weight.astype(jnp.bfloat16), "dp", axis=1, tiled=True),
        lax.all_gather(up_weight.astype(jnp.bfloat16), "dp", axis=0, tiled=True),
        lax.all_gather(down_weight.astype(jnp.bfloat16), "dp", axis=2, tiled=True),
        lax.all_gather(time_inner.astype(jnp.bfloat16), "dp", axis=0, tiled=True),
        lax.all_gather(time_outer.astype(jnp.bfloat16), "dp", axis=0, tiled=True),
        lax.all_gather(time_bias.astype(jnp.bfloat16), "dp", axis=0, tiled=True),
        lax.all_gather(head_vectors.astype(jnp.bfloat16), "dp", axis=2, tiled=True),
        lax.all_gather(layer_vectors.astype(jnp.bfloat16), "dp", axis=1, tiled=True),
    )
    local_width = w_out.shape[0]
    head_count = local_width // HD
    packed = tokens.shape[0]
    head_rows = head_vec.astype(jnp.float32).reshape(6, local_width)
    layer_rows = layer_vec.astype(jnp.float32)
    score_scale = 1.0 / math.sqrt(HD)
    block_rows = min(PACK, 512)
    block_count = packed // block_rows
    seg_row = segment_ids[0]
    features = time_features(timesteps[0], TD)
    feature_low = features.astype(jnp.bfloat16)
    inner_pre = jnp.dot(feature_low, w_inner, preferred_element_type=jnp.float32) + b_inner.astype(
        jnp.float32
    )
    silu_out, silu_pull = jax.vjp(jax.nn.silu, inner_pre)
    act_low = silu_out.astype(jnp.bfloat16)
    time_embed = jnp.dot(act_low, w_outer, preferred_element_type=jnp.float32) + layer_rows[6]
    onehot = (seg_row[:, None] == jnp.arange(SEGS, dtype=jnp.int32)[None, :]).astype(jnp.float32)
    hidden0 = tokens.astype(jnp.float32) + jnp.dot(
        onehot, time_embed, precision=lax.Precision.HIGHEST, preferred_element_type=jnp.float32
    )
    hidden_low = hidden0.astype(jnp.bfloat16)
    projected = jnp.einsum("pd,dce->pce", hidden_low, w_qkv, preferred_element_type=jnp.float32)
    queries = (projected[:, 0] + head_rows[0]).astype(jnp.bfloat16)
    keys_low = projected[:, 1].astype(jnp.bfloat16)
    values_low = (projected[:, 2] + head_rows[1]).astype(jnp.bfloat16)

    def block_scores(query_blk, key_all, seg_query):
        raw_scores = (
            jnp.einsum("qd,kd->qk", query_blk, key_all, preferred_element_type=jnp.float32)
            * score_scale
        )
        same_doc = seg_query[:, None] == seg_row[None, :]
        return (raw_scores, same_doc)

    def attend_head(head_index):
        query_h = head_slice(queries, head_index)
        key_h = head_slice(keys_low, head_index)
        value_h = head_slice(values_low, head_index)
        out_blocks = []
        sum_blocks = []
        for block_index in range(block_count):
            first_row = block_index * block_rows
            raw_scores, same_doc = block_scores(
                query_h[first_row : first_row + block_rows],
                key_h,
                seg_row[first_row : first_row + block_rows],
            )
            masked = jnp.where(same_doc, raw_scores, -1e30)
            row_peak = jnp.max(masked, axis=1, keepdims=True)
            exponent = jnp.exp(masked - row_peak)
            row_total = jnp.sum(exponent, axis=1, keepdims=True)
            soft_weights = exponent / row_total
            out_blocks.append(
                jnp.dot(
                    soft_weights.astype(jnp.bfloat16), value_h, preferred_element_type=jnp.float32
                )
            )
            sum_blocks.append((row_peak + jnp.log(row_total))[:, 0])
        return (jnp.concatenate(out_blocks, axis=0), jnp.concatenate(sum_blocks, axis=0))

    head_out, log_sums = lax.map(attend_head, jnp.arange(head_count, dtype=jnp.int32))
    att_low = merge_heads(head_out).astype(jnp.bfloat16)
    attn_partial = jnp.dot(att_low, w_out, preferred_element_type=jnp.float32)
    attn_branch = (
        lax.psum(attn_partial.astype(jnp.bfloat16), "tensor").astype(jnp.float32) + layer_rows[0]
    )
    residual1 = hidden0 + attn_branch
    cot_here = cotangent.astype(jnp.float32)
    normed1, norm1_pull = jax.vjp(layer_norm, residual1, layer_rows[1], layer_rows[2])
    norm_here = normed1.astype(jnp.bfloat16)
    up_pre = (
        jnp.einsum("pd,dje->pje", norm_here, w_up, preferred_element_type=jnp.float32)
        + head_rows[2:]
    )
    gelu_out, gelu_pull = jax.vjp(gelu_exact, up_pre)
    hid_low = gelu_out.astype(jnp.bfloat16)
    down_partial = jnp.einsum("pje,jef->pf", hid_low, w_down, preferred_element_type=jnp.float32)
    mlp_branch = (
        lax.psum(down_partial.astype(jnp.bfloat16), "tensor").astype(jnp.float32) + layer_rows[3]
    )
    result, norm2_pull = jax.vjp(layer_norm, normed1 + mlp_branch, layer_rows[4], layer_rows[5])
    output_here = result.astype(jnp.bfloat16)
    back_r2, back_gain2, back_shift2 = norm2_pull(cot_here)
    part_bdown = jnp.sum(back_r2, axis=0)
    back_r2_here = back_r2.astype(jnp.bfloat16)
    grad_down = jnp.einsum("pje,pf->jef", hid_low, back_r2_here, preferred_element_type=jnp.float32)
    back_hid = jnp.einsum("pf,jef->pje", back_r2_here, w_down, preferred_element_type=jnp.float32)
    (back_up,) = gelu_pull(back_hid)
    grad_bup = jnp.sum(back_up, axis=0)
    back_up_low = back_up.astype(jnp.bfloat16)
    grad_up = jnp.einsum("pd,pje->dje", norm_here, back_up_low, preferred_element_type=jnp.float32)
    back_a_part = jnp.einsum("pje,dje->pd", back_up_low, w_up, preferred_element_type=jnp.float32)
    back_a = lax.psum(back_a_part.astype(jnp.bfloat16), "tensor").astype(jnp.float32) + back_r2
    back_r1, back_gain1, back_shift1 = norm1_pull(back_a)
    grad_bout = jnp.sum(back_r1, axis=0)
    back_r1_low = back_r1.astype(jnp.bfloat16)
    grad_out = jnp.einsum("pe,pf->ef", att_low, back_r1_low, preferred_element_type=jnp.float32)
    back_att = jnp.einsum(
        "pf,ef->pe", back_r1_low, w_out, preferred_element_type=jnp.float32
    ).astype(jnp.bfloat16)

    def head_back(head_index):
        query_h = head_slice(queries, head_index)
        key_h = head_slice(keys_low, head_index)
        value_h = head_slice(values_low, head_index)
        grad_h = head_slice(back_att, head_index)
        lse_h = log_sums[head_index]
        key_grad = jnp.zeros((packed, HD), jnp.float32)
        value_grad = jnp.zeros((packed, HD), jnp.float32)
        query_blocks = []
        for block_index in range(block_count):
            first_row = block_index * block_rows
            query_blk = query_h[first_row : first_row + block_rows]
            raw_scores, same_doc = block_scores(
                query_blk, key_h, seg_row[first_row : first_row + block_rows]
            )
            lse_blk = lse_h[first_row : first_row + block_rows]
            soft_weights = jnp.where(same_doc, jnp.exp(raw_scores - lse_blk[:, None]), 0.0)
            grad_blk = grad_h[first_row : first_row + block_rows]
            value_grad = value_grad + jnp.einsum(
                "qk,qd->kd",
                soft_weights.astype(jnp.bfloat16),
                grad_blk,
                preferred_element_type=jnp.float32,
            )
            weight_grad = jnp.einsum(
                "qd,kd->qk", grad_blk, value_h, preferred_element_type=jnp.float32
            )
            row_inner = jnp.sum(soft_weights * weight_grad, axis=1, keepdims=True)
            score_low = (soft_weights * (weight_grad - row_inner)).astype(jnp.bfloat16)
            query_blocks.append(
                jnp.dot(score_low, key_h, preferred_element_type=jnp.float32) * score_scale
            )
            key_grad = (
                key_grad
                + jnp.einsum("qk,qd->kd", score_low, query_blk, preferred_element_type=jnp.float32)
                * score_scale
            )
        return (jnp.concatenate(query_blocks, axis=0), key_grad, value_grad)

    query_grads, key_grads, value_grads = lax.map(
        head_back, jnp.arange(head_count, dtype=jnp.int32)
    )
    query_grad_all = merge_heads(query_grads)
    key_grad_all = merge_heads(key_grads)
    value_grad_all = merge_heads(value_grads)
    grad_bq = jnp.sum(query_grad_all, axis=0)
    grad_bv = jnp.sum(value_grad_all, axis=0)
    proj_grad_low = jnp.stack([query_grad_all, key_grad_all, value_grad_all], axis=1).astype(
        jnp.bfloat16
    )
    grad_qkv = jnp.einsum(
        "pd,pce->dce", hidden_low, proj_grad_low, preferred_element_type=jnp.float32
    )
    back_h_part = jnp.einsum(
        "pce,dce->pd", proj_grad_low, w_qkv, preferred_element_type=jnp.float32
    )
    back_h0 = lax.psum(back_h_part.astype(jnp.bfloat16), "tensor").astype(jnp.float32) + back_r1
    input_grad = back_h0.astype(jnp.bfloat16)
    back_time = jnp.einsum(
        "ps,pd->sd",
        onehot,
        back_h0,
        precision=lax.Precision.HIGHEST,
        preferred_element_type=jnp.float32,
    )
    grad_bouter = jnp.sum(back_time, axis=0)
    back_time_low = back_time.astype(jnp.bfloat16)
    grad_outer = jnp.einsum("su,sd->ud", act_low, back_time_low, preferred_element_type=jnp.float32)
    back_act = jnp.einsum("sd,ud->su", back_time_low, w_outer, preferred_element_type=jnp.float32)
    (back_inner,) = silu_pull(back_act)
    grad_binner = jnp.sum(back_inner, axis=0)
    grad_inner = jnp.einsum(
        "st,su->tu",
        feature_low,
        back_inner.astype(jnp.bfloat16),
        preferred_element_type=jnp.float32,
    )
    grad_head = jnp.concatenate([grad_bq[None], grad_bv[None], grad_bup], axis=0).reshape(
        6, 1, local_width
    )
    grad_layer = jnp.stack(
        [grad_bout, back_gain1, back_shift1, part_bdown, back_gain2, back_shift2, grad_bouter],
        axis=0,
    )
    red_qkv, red_out, red_up, red_down, red_inner, red_outer, red_binner, red_head, red_layer = (
        lax.psum_scatter(grad_qkv, "dp", scatter_dimension=0, tiled=True),
        lax.psum_scatter(grad_out, "dp", scatter_dimension=1, tiled=True),
        lax.psum_scatter(grad_up, "dp", scatter_dimension=0, tiled=True),
        lax.psum_scatter(grad_down, "dp", scatter_dimension=2, tiled=True),
        lax.psum_scatter(grad_inner, "dp", scatter_dimension=0, tiled=True),
        lax.psum_scatter(grad_outer, "dp", scatter_dimension=0, tiled=True),
        lax.psum_scatter(grad_binner, "dp", scatter_dimension=0, tiled=True),
        lax.psum_scatter(grad_head, "dp", scatter_dimension=2, tiled=True),
        lax.psum_scatter(grad_layer, "dp", scatter_dimension=1, tiled=True),
    )
    split_squares = sum(
        (jnp.sum(piece * piece) for piece in (red_qkv, red_out, red_up, red_down, red_head))
    )
    shared_squares = sum(
        (jnp.sum(piece * piece) for piece in (red_inner, red_outer, red_binner, red_layer))
    )
    local_squares = split_squares + shared_squares / lax.axis_size("tensor")
    norm = jnp.sqrt(lax.psum(local_squares, ("dp", "tensor")))
    factor = 1.0 / jnp.maximum(norm, 1.0)
    step_rate = 4.0 * math.sqrt(MPARAMS / D)
    qkv_master, qkv_velocity, qkv_smoothed = advance(
        qkv_weight, qkv_moment, qkv_average, red_qkv, factor, step_rate
    )
    out_master, out_velocity, out_smoothed = advance(
        out_weight, out_moment, out_average, red_out, factor, step_rate
    )
    up_master, up_velocity, up_smoothed = advance(
        up_weight, up_moment, up_average, red_up, factor, step_rate
    )
    down_master, down_velocity, down_smoothed = advance(
        down_weight, down_moment, down_average, red_down, factor, step_rate
    )
    inner_master, inner_velocity, inner_smoothed = advance(
        time_inner, inner_moment, inner_average, red_inner, factor, step_rate
    )
    outer_master, outer_velocity, outer_smoothed = advance(
        time_outer, outer_moment, outer_average, red_outer, factor, step_rate
    )
    bias_master, bias_velocity, bias_smoothed = advance(
        time_bias, bias_moment, bias_average, red_binner, factor, step_rate
    )
    head_master, head_velocity, head_smoothed = advance(
        head_vectors, head_moment, head_average, red_head, factor, step_rate
    )
    layer_master, layer_velocity, layer_smoothed = advance(
        layer_vectors, layer_moment, layer_average, red_layer, factor, step_rate
    )
    return (
        output_here,
        input_grad,
        norm,
        qkv_master,
        out_master,
        up_master,
        down_master,
        inner_master,
        outer_master,
        bias_master,
        head_master,
        layer_master,
        qkv_velocity,
        out_velocity,
        up_velocity,
        down_velocity,
        inner_velocity,
        outer_velocity,
        bias_velocity,
        head_velocity,
        layer_velocity,
        qkv_smoothed,
        out_smoothed,
        up_smoothed,
        down_smoothed,
        inner_smoothed,
        outer_smoothed,
        bias_smoothed,
        head_smoothed,
        layer_smoothed,
    )


def solution(mesh):
    return jax.shard_map(
        shards,
        mesh=mesh,
        in_specs=(
            P("dp", None),
            P("dp", None),
            P("dp", None),
            P("dp", None),
            P("dp", None, "tensor"),
            P("tensor", "dp"),
            P("dp", None, "tensor"),
            P(None, "tensor", "dp"),
            P("dp", None),
            P("dp", None),
            P("dp"),
            P(None, "tensor", "dp"),
            P(None, "dp"),
            P("dp", None, "tensor"),
            P("tensor", "dp"),
            P("dp", None, "tensor"),
            P(None, "tensor", "dp"),
            P("dp", None),
            P("dp", None),
            P("dp"),
            P(None, "tensor", "dp"),
            P(None, "dp"),
            P("dp", None, "tensor"),
            P("tensor", "dp"),
            P("dp", None, "tensor"),
            P(None, "tensor", "dp"),
            P("dp", None),
            P("dp", None),
            P("dp"),
            P(None, "tensor", "dp"),
            P(None, "dp"),
        ),
        out_specs=(
            P("dp", None),
            P("dp", None),
            P(),
            P("dp", None, "tensor"),
            P("tensor", "dp"),
            P("dp", None, "tensor"),
            P(None, "tensor", "dp"),
            P("dp", None),
            P("dp", None),
            P("dp"),
            P(None, "tensor", "dp"),
            P(None, "dp"),
            P("dp", None, "tensor"),
            P("tensor", "dp"),
            P("dp", None, "tensor"),
            P(None, "tensor", "dp"),
            P("dp", None),
            P("dp", None),
            P("dp"),
            P(None, "tensor", "dp"),
            P(None, "dp"),
            P("dp", None, "tensor"),
            P("tensor", "dp"),
            P("dp", None, "tensor"),
            P(None, "tensor", "dp"),
            P("dp", None),
            P("dp", None),
            P("dp"),
            P(None, "tensor", "dp"),
            P(None, "dp"),
        ),
        check_vma=False,
    )
```

profile of v0, /device:TPU:0, one launch (start us, length us, event | category | flops | bytes accessed | tf_op | source)
XLA Modules:
  0.0 1384.8 jit_solution(9287977325639538322)
XLA Ops:
  9.7 23.1 %all-gather = bf16[16,48,7]{1,2,0:T(8,128)(2,1)S(1)} all-gather(bf16[1,48,7]{1,2,0:T(8,128)(2,1)S(1)} %convert_bitcast_fusion), channel_id=1, replica_groups=mesh['dp'=16,'tensor'=2] {'dp'}, dimensions={0}, use_global_device_ids=true | all-gather | bytes 11424 | tf_op jit(solution)/shard_map/all_gather | solution.py:97
  38.2 29.9 %all-reduce = bf16[512]{0:T(512)(128)(2,1)S(1)} all-reduce(bf16[512]{0:T(512)(128)(2,1)S(1)} %dynamic-update-slice), channel_id=1, replica_groups=mesh['dp'=16,'tensor'=2] {'dp'}, use_global_device_ids=true, to_apply=%add | all-reduce | flops 512 | bytes 2048
  71.0 17.6 %all_gather.32 = bf16[6,1,384]{0,1,2:T(2,128)(2,1)S(1)} all-gather(bf16[6,1,24]{0,1,2:T(2,128)(2,1)S(1)} %copy.156), channel_id=1, replica_groups=mesh['dp'=16,'tensor'=2] {'dp'}, dimensions={2}, use_global_device_ids=true | all-gather | bytes 4896 | tf_op jit(solution)/shard_map/all_gather | solution.py:96
  89.5 19.5 %all_gather.27 = bf16[128,512]{1,0:T(8,128)(2,1)S(1)} all-gather(bf16[8,512]{1,0:T(8,128)(2,1)S(1)} %convert_element_type.164), channel_id=1, replica_groups=mesh['dp'=16,'tensor'=2] {'dp'}, dimensions={0}, use_global_device_ids=true | all-gather | bytes 139264 | tf_op jit(solution)/shard_map/all_gather | solution.py:93
  111.7 19.6 %all_gather.29 = bf16[512,768]{1,0:T(8,128)(2,1)S(1)} all-gather(bf16[32,768]{1,0:T(8,128)(2,1)S(1)} %convert_element_type.168), channel_id=1, replica_groups=mesh['dp'=16,'tensor'=2] {'dp'}, dimensions={0}, use_global_device_ids=true | all-gather | bytes 835584 | tf_op jit(solution)/shard_map/all_gather | solution.py:94
  132.4 22.2 %all_gather.33 = bf16[384,768]{0,1:T(8,128)(2,1)} all-gather(bf16[384,48]{0,1:T(8,128)(2,1)S(1)} %convert_element_type.181), channel_id=1, replica_groups=mesh['dp'=16,'tensor'=2] {'dp'}, dimensions={1}, use_global_device_ids=true | all-gather | bytes 626688 | tf_op jit(solution)/shard_map/all_gather | solution.py:90
  159.0 5.7 fusion.101
  165.7 94.4 %while.28 = (s32[]{:T(128)}, bf16[6,1536,64]{1,2,0:T(8,128)(2,1)}, f32[6,1536]{1,0:T(8,128)}, s32[1536]{0:T(1024)S(1)}, s32[1,1536]{1,0:T(1,128)}, /*index=5*/s3...) while((s32[]{:T(128)}, bf16[6,1536,64]{1,2,0:T(8,128)(2,1)}, ...), condition=%wide.region_7.8_spmd.clone, body=%wide.region_0.7_spmd.sunk.clone | while | flops 625804800 | bytes 32123292 | solution.py:160
  272.0 58.5 %all-reduce.9.cloned.1.call-done = bf16[1536,768]{0,1:T(8,128)(2,1)} async-done(((bf16[1536,768]{0,1:T(8,128)(2,1)}), bf16[1536,768]{0,1:T(8,128)(2,1)}) %all-reduce.9.cloned.1.call-update) | async-done | bytes 2359312 | tf_op jit(solution)/shard_map/psum | solution.py:164
  338.2 37.8 %all-gather.7.cloned.1.call-done = bf16[768,4,384]{2,0,1:T(8,128)(2,1)} async-done(((bf16[48,4,384]{2,0,1:T(8,128)(2,1)}), bf16[768,4,384]{2,0,1:T(8,128)(2,1)}) %all-gather.7.cloned.1.call-update) | async-done | bytes 2359312 | tf_op jit(solution)/shard_map/all_gather | solution.py:91
  375.9 10.1 fusion.108
  389.6 22.9 %multiply_convert_fusion.3 = (bf16[1536,4,384]{2,0,1:T(8,128)(2,1)}, f32[1536,4,384]{2,0,1:T(8,128)}) fusion(f32[1536,4,384]{2,0,1:T(8,128)S(1)} %get-tuple-element.430, f32[4,384]{1,0:T(4,128)S(1)} %copy-done.71, u8[1536,384]{1,0:T(8,128)(4,1)S(1)} %get-tuple-element.300, u8[1536,384]{1,0:T(8,128)(4,1)S(1)} %get-tuple-element.299), kind=kLoop, calls=%fused_computation.120 | loop fusion | flops 167510016 | bytes 24778752 | tf_op jit(solution)/shard_map/convert_element_type | solution.py:175
  412.5 7.5 all-gather.9.cloned.1.call-done
  420.0 8.4 bitcast_convert_fusion.2
  432.9 63.1 %all-reduce.11.cloned.1.call-done = bf16[1536,768]{0,1:T(8,128)(2,1)} async-done(((bf16[1536,768]{0,1:T(8,128)(2,1)}), bf16[1536,768]{0,1:T(8,128)(2,1)}) %all-reduce.11.cloned.1.call-update) | async-done | bytes 2359312 | tf_op jit(solution)/shard_map/psum | solution.py:178
  507.4 14.0 %fusion.154 = (f32[4,384]{1,0:T(4,128)}, bf16[1536,4,384]{2,0,1:T(8,128)(2,1)S(1)}) fusion(f32[1536,4,384]{2,0,1:T(8,128)} %get-tuple-element.392, bf16[4,384,768]{1,2,0:T(8,128)(2,1)S(1)} %copy-done.96, f32[1536,768]{0,1:T(8,128)S(1)} %get-tuple-element.388, f32[1536]{0:T(1024)S(1)} %negate_multiply_fusion.2, f32[1536,4,384]{2,0,1:T(8,128)} %copy-done.13, ...), kind=kOutput, calls=%fused_computation.296 | convolution fusion | flops 3663985152 | bytes 30689280 | tf_op jit(solution)/shard_map/pf,jef->pje/dot_general | solution.py:186
  528.7 68.7 %all-reduce.13.cloned.1.call-done = bf16[1536,768]{0,1:T(8,128)(2,1)} async-done(((bf16[1536,768]{0,1:T(8,128)(2,1)}), bf16[1536,768]{0,1:T(8,128)(2,1)}) %all-reduce.13.cloned.1.call-update) | async-done | bytes 2359312 | tf_op jit(solution)/shard_map/psum | solution.py:192
  597.4 7.5 multiply_reduce_fusion.3
  612.9 151.7 %while.29 = (s32[]{:T(128)}, f32[6,1536,64]{1,2,0:T(8,128)}, bf16[6,1536,64]{1,2,0:T(8,128)(2,1)}, f32[6,1536,64]{1,2,0:T(8,128)}, s32[1536]{0:T(1024)S(1)}, /*i...) while((s32[]{:T(128)}, f32[6,1536,64]{1,2,0:T(8,128)}, ...), condition=%wide.region_23.24_spmd.clone, body=%wide.region_19.23_spmd.sunk.clone | while | flops 1534327296 | bytes 114141736 | solution.py:240
  771.2 6.9 bitcast_convert_fusion
  783.2 63.7 %all-reduce.15.cloned.1.call-done = bf16[1536,768]{0,1:T(8,128)(2,1)} async-done(((bf16[1536,768]{0,1:T(8,128)(2,1)}), bf16[1536,768]{0,1:T(8,128)(2,1)}) %all-reduce.15.cloned.1.call-update) | async-done | bytes 2359312 | tf_op jit(solution)/shard_map/psum | solution.py:257
  860.5 10.0 fusion.104
  871.2 9.7 fusion.117
  882.2 8.0 fusion.99
  898.7 10.1 reduce-scatter.13.cloned.1.call-done
  910.3 57.7 %all-reduce.3 = (f32[6,1,384]{2,1,0:T(1,128)S(1)}, f32[512]{0:T(512)S(1)}) all-reduce(f32[6,1,384]{2,1,0:T(1,128)S(1)} %reshape.199, f32[512]{0:T(512)S(1)} %get-tuple-element.433), channel_id=6, replica_groups=mesh['dp'=16,'tensor'=2] {'dp'}, use_global_device_ids=true, to_apply=%region_36.37.clone | all-reduce | flops 2816 | bytes 22528
  970.7 54.9 %reduce-scatter.19.cloned.1.call-done = f32[8,512]{1,0:T(8,128)} async-done(((f32[128,512]{1,0:T(8,128)}), f32[8,512]{1,0:T(8,128)}) %reduce-scatter.19.cloned.1.call-update) | async-done | bytes 16400 | tf_op jit(solution)/shard_map/reduce_scatter | solution.py:290
  1027.0 61.4 %reduce-scatter.21.cloned.1.call-done = f32[32,768]{1,0:T(8,128)} async-done(((f32[512,768]{1,0:T(8,128)}), f32[32,768]{1,0:T(8,128)}) %reduce-scatter.21.cloned.1.call-update) | async-done | bytes 98320 | tf_op jit(solution)/shard_map/reduce_scatter | solution.py:291
  1092.5 74.2 %reduce-scatter.15.cloned.1.call-done = f32[48,4,384]{2,0,1:T(8,128)} async-done(((f32[768,4,384]{2,0,1:T(8,128)}), f32[48,4,384]{2,0,1:T(8,128)}) %reduce-scatter.15.cloned.1.call-update) | async-done | bytes 294928 | tf_op jit(solution)/shard_map/reduce_scatter | solution.py:288
  1168.3 77.2 %reduce-scatter.17.cloned.1.call-done = f32[4,384,48]{1,2,0:T(8,128)} async-done(((f32[4,384,768]{1,2,0:T(8,128)}), f32[4,384,48]{1,2,0:T(8,128)}) %reduce-scatter.17.cloned.1.call-update) | async-done | bytes 294928 | tf_op jit(solution)/shard_map/reduce_scatter | solution.py:289
  1247.2 69.2 %reduce-scatter.11.cloned.1.call-done = f32[48,3,384]{2,0,1:T(8,128)} async-done(((f32[768,3,384]{2,0,1:T(8,128)}), f32[48,3,384]{2,0,1:T(8,128)}) %reduce-scatter.11.cloned.1.call-update) | async-done | bytes 221200 | tf_op jit(solution)/shard_map/reduce_scatter | solution.py:286
  1323.8 39.6 %psum.39 = f32[]{:T(128)} all-reduce(f32[]{:T(128)S(6)} %add.362), channel_id=1, replica_groups=mesh['dp'=16,'tensor'=2] {'dp','tensor'}, use_global_device_ids=true, to_apply=%region_54.55 | all-reduce | flops 1 | bytes 8 | tf_op jit(solution)/shard_map/psum | solution.py:303
  (739 shorter events, 359.8 us)
Async XLA Ops:
  7.3 61.6 %copy-start.36 = (f32[384,48]{0,1:T(8,128)S(1)}, f32[384,48]{0,1:T(8,128)}, u32[]{:S(2)}) copy-start(f32[384,48]{0,1:T(8,128)} %param.40) | copy-start | bytes 221188
  7.3 151.7 %all-gather.5.cloned.1.call-start = ((), (), s32[]{:S(2)}) async-start(), calls=%async_computation.7 | async-start | bytes 1880064 | tf_op jit(solution)/shard_map/all_gather | solution.py:89
  9.0 321.5 %all-reduce.9.cloned.1.call-start = ((), (), s32[]{:S(2)}) async-start(), calls=%async_computation.8 | async-start | bytes 4718592 | tf_op jit(solution)/shard_map/psum | solution.py:164
  36.6 74.8 %copy-start.97 = (s32[1,2]{1,0:T(1,128)S(1)}, s32[1,2]{1,0:T(1,128)}, u32[]{:S(2)}) copy-start(s32[1,2]{1,0:T(1,128)} %param.38) | copy-start | bytes 28
  264.3 66.2 %copy-start.75 = (f32[768]{0:T(1024)S(1)}, f32[768]{0:T(1024)}, u32[]{:S(2)}) copy-start(f32[768]{0:T(1024)} %get-tuple-element.313) | copy-start | bytes 9220
  264.3 111.6 %all-gather.7.cloned.1.call-start = ((), (), s32[]{:S(2)}) async-start(), calls=%async_computation.9 | async-start | bytes 2506752 | tf_op jit(solution)/shard_map/all_gather | solution.py:91
  266.0 154.0 %all-gather.9.cloned.1.call-start = ((), (), s32[]{:S(2)}) async-start(), calls=%async_computation.10 | async-start | bytes 2506752 | tf_op jit(solution)/shard_map/all_gather | solution.py:92
  267.8 228.2 %all-reduce.11.cloned.1.call-start = ((), (), s32[]{:S(2)}) async-start(), calls=%async_computation.11 | async-start | bytes 4718592 | tf_op jit(solution)/shard_map/psum | solution.py:178
  334.3 270.7 %copy-start.48 = (f32[1536]{0:T(1024)}, f32[1536]{0:T(1024)S(1)}, u32[]{:S(2)}) copy-start(f32[1536]{0:T(1024)S(1)} %broadcast_multiply_fusion.1) | copy-start | bytes 18436
  428.4 169.0 %all-reduce.13.cloned.1.call-start = ((), (), s32[]{:S(2)}) async-start(), calls=%async_computation.12 | async-start | bytes 4718592 | tf_op jit(solution)/shard_map/psum | solution.py:192
  528.6 318.3 %all-reduce.15.cloned.1.call-start = ((), (), s32[]{:S(2)}) async-start(), calls=%async_computation.13 | async-start | bytes 4718592 | tf_op jit(solution)/shard_map/psum | solution.py:257
  778.2 130.6 %reduce-scatter.13.cloned.1.call-start = ((), (), s32[]{:S(2)}) async-start(), calls=%async_computation.15 | async-start | bytes 1253376 | tf_op jit(solution)/shard_map/reduce_scatter | solution.py:287
  783.1 186.3 %reduce-scatter.23.cloned.1.call-start = ((), (), s32[]{:S(2)}) async-start(), calls=%async_computation.20 | async-start | bytes 417792
  857.7 168.0 %reduce-scatter.19.cloned.1.call-start = ((), (), s32[]{:S(2)}) async-start(), calls=%async_computation.18 | async-start | bytes 278528 | tf_op jit(solution)/shard_map/reduce_scatter | solution.py:290
  858.8 229.6 %reduce-scatter.21.cloned.1.call-start = ((), (), s32[]{:S(2)}) async-start(), calls=%async_computation.19 | async-start | bytes 1671168 | tf_op jit(solution)/shard_map/reduce_scatter | solution.py:291
  860.4 306.2 %reduce-scatter.15.cloned.1.call-start = ((), (), s32[]{:S(2)}) async-start(), calls=%async_computation.16 | async-start | bytes 5013504 | tf_op jit(solution)/shard_map/reduce_scatter | solution.py:288
  870.5 375.1 %reduce-scatter.17.cloned.1.call-start = ((), (), s32[]{:S(2)}) async-start(), calls=%async_computation.17 | async-start | bytes 5013504 | tf_op jit(solution)/shard_map/reduce_scatter | solution.py:289
  880.9 435.5 %reduce-scatter.11.cloned.1.call-start = ((), (), s32[]{:S(2)}) async-start(), calls=%async_computation.14 | async-start | bytes 3760128 | tf_op jit(solution)/shard_map/reduce_scatter | solution.py:286
  898.5 465.6 %copy-start.20 = (f32[48,4,384]{2,1,0:T(4,128)S(1)}, f32[48,4,384]{2,1,0:T(4,128)}, u32[]{:S(2)}) copy-start(f32[48,4,384]{2,1,0:T(4,128)} %param.41) | copy-start | bytes 884740
  968.0 124.5 %copy-start.91 = (f32[6,1,384]{2,1,0:T(1,128)}, f32[6,1,384]{2,1,0:T(1,128)S(1)}, u32[]{:S(2)}) copy-start(f32[6,1,384]{2,1,0:T(1,128)S(1)} %get-tuple-element.357) | copy-start | bytes 27652
  968.0 124.5 %copy-start.94 = (f32[512]{0:T(512)}, f32[512]{0:T(512)S(1)}, u32[]{:S(2)}) copy-start(f32[512]{0:T(512)S(1)} %get-tuple-element.358) | copy-start | bytes 6148
  1166.6 197.5 %copy-start.23 = (f32[48,4,384]{2,0,1:T(8,128)S(1)}, f32[48,4,384]{2,0,1:T(8,128)}, u32[]{:S(2)}) copy-start(f32[48,4,384]{2,0,1:T(8,128)} %reduce-scatter.15.cloned.1.call-done) | copy-start | bytes 884740
  1321.3 49.4 %copy-start.83 = (f32[7,48]{1,0:T(8,128)S(1)}, f32[7,48]{1,0:T(8,128)}, u32[]{:S(2)}) copy-start(f32[7,48]{1,0:T(8,128)} %param.47) | copy-start | bytes 4036
  1321.3 49.4 %copy-start.90 = (f32[7,48]{1,0:T(8,128)S(1)}, f32[7,48]{1,0:T(8,128)}, u32[]{:S(2)}) copy-start(f32[7,48]{1,0:T(8,128)} %param.65) | copy-start | bytes 4036
  1321.3 50.7 %copy-start.28 = (f32[48,3,384]{2,0,1:T(8,128)S(1)}, f32[48,3,384]{2,0,1:T(8,128)}, u32[]{:S(2)}) copy-start(f32[48,3,384]{2,0,1:T(8,128)} %reduce-scatter.11.cloned.1.call-done) | copy-start | bytes 663556
  1321.3 50.7 %copy-start.29 = (f32[48,3,384]{2,0,1:T(8,128)S(1)}, f32[48,3,384]{2,0,1:T(8,128)}, u32[]{:S(2)}) copy-start(f32[48,3,384]{2,0,1:T(8,128)} %param.39) | copy-start | bytes 663556
  1323.8 49.1 %copy-start.38 = (f32[384,48]{0,1:T(8,128)S(1)}, f32[384,48]{0,1:T(8,128)}, u32[]{:S(2)}) copy-start(f32[384,48]{0,1:T(8,128)} %reduce-scatter.13.cloned.1.call-done) | copy-start | bytes 221188
  1323.8 49.1 %copy-start.56 = (f32[384,48]{0,1:T(8,128)S(1)}, f32[384,48]{0,1:T(8,128)}, u32[]{:S(2)}) copy-start(f32[384,48]{0,1:T(8,128)} %param.58) | copy-start | bytes 221188
  1323.8 50.7 %copy-start.21 = (f32[4,384,48]{1,2,0:T(8,128)S(1)}, f32[4,384,48]{1,2,0:T(8,128)}, u32[]{:S(2)}) copy-start(f32[4,384,48]{1,2,0:T(8,128)} %param.42) | copy-start | bytes 884740
  1323.8 50.7 %copy-start.22 = (f32[4,384,48]{1,2,0:T(8,128)S(1)}, f32[4,384,48]{1,2,0:T(8,128)}, u32[]{:S(2)}) copy-start(f32[4,384,48]{1,2,0:T(8,128)} %reduce-scatter.17.cloned.1.call-done) | copy-start | bytes 884740
  1323.8 50.7 %copy-start.34 = (f32[4,384,48]{1,2,0:T(8,128)S(1)}, f32[4,384,48]{1,2,0:T(8,128)}, u32[]{:S(2)}) copy-start(f32[4,384,48]{1,2,0:T(8,128)} %param.60) | copy-start | bytes 884740
  1323.8 50.7 %copy-start.35 = (f32[4,384,48]{1,2,0:T(8,128)S(1)}, f32[4,384,48]{1,2,0:T(8,128)}, u32[]{:S(2)}) copy-start(f32[4,384,48]{1,2,0:T(8,128)} %param.51) | copy-start | bytes 884740
  (161 other events, 834.5 us)
Sparse Core Ops, SparseCore 0:
  11.0 43.2 all-gather.4
  264.4 65.9 all-reduce.8
  333.5 42.4 all-gather.6
  378.8 41.1 all-gather.8
  428.5 67.4 all-reduce.10
  528.8 68.6 all-reduce.12
  778.3 68.6 all-reduce.14
  850.6 58.1 reduce-scatter.12
  912.3 54.5 reduce-scatter.22
  971.2 54.3 reduce-scatter.18
  1029.8 58.5 reduce-scatter.20
  1092.0 74.5 reduce-scatter.14
  1171.0 74.5 reduce-scatter.16
  1249.3 67.0 reduce-scatter.10
where the time goes:
time: 1390 us; the launch traced here: 1380 us
  waiting for transfers between devices  646 us (46%)
  matrix products  246 us (18%)
  blocking collectives  229 us (16%)
  other arithmetic  124 us (9%)
  local copies, waits for them, and re-layouts  90.9 us (7%)
  between operations  25 us (2%)
  loops' own time  21.4 us (2%)
    unnamed x2, blocking collectives  87.6 us
    reduce_scatter x1, waiting for transfers between devices, shards(): lax.psum_scatter(grad_down, 'dp', scatter_dimension=2, tiled=True)  77.2 us
    reduce_scatter x1, waiting for transfers between devices, shards(): lax.psum_scatter(grad_up, 'dp', scatter_dimension=0, tiled=True)  74.2 us
    reduce_scatter x1, waiting for transfers between devices, shards(): lax.psum_scatter(grad_qkv, 'dp', scatter_dimension=0, tiled=True)  69.2 us
    psum x1, waiting for transfers between devices, shards(): lax.psum(back_a_part.astype(jnp.bfloat16), 'tensor').astype(jnp.float32)  68.7 us
    psum x1, waiting for transfers between devices, shards(): lax.psum(back_h_part.astype(jnp.bfloat16), 'tensor').astype(jnp.float32)  63.7 us
    psum x1, waiting for transfers between devices, shards(): lax.psum(down_partial.astype(jnp.bfloat16), 'tensor').astype(jnp.float32)  63.1 us
    reduce_scatter x1, waiting for transfers between devices, shards(): lax.psum_scatter(grad_outer, 'dp', scatter_dimension=0, tiled=True)  61.4 us
  transfers between devices with their start and end apart: 14, of which 12 were waited for; matrix products, arithmetic and copies ran while one was open for 9% of the time, Pallas kernels for 0%

commit v1 on v0

--- a/solution.py
+++ b/solution.py
@@ -1,8 +1,11 @@
+import functools
 import math
 
 import jax
 import jax.numpy as jnp
 from jax import lax
+from jax.experimental import pallas as pl
+from jax.experimental.pallas import tpu as pltpu
 from jax.sharding import PartitionSpec as P
 
 D = 768
@@ -52,7 +55,7 @@
     return (fresh_master, velocity, smoothed)
 
 
-def shards(
+def shards_any(
     tokens,
     cotangent,
     segment_ids,
@@ -364,9 +367,386 @@
     )
 
 
+F32=jnp.float32; BF=jnp.bfloat16
+MESH=pl.DeviceIdType.MESH
+NZ,NX,NC,NT=4,2,2,2
+ROWS=48; PIECE=384
+
+def place():
+    dp=lax.axis_index("dp"); t=lax.axis_index("tensor")
+    z=lax.div(dp,4); x=lax.rem(lax.div(dp,2),2); c=lax.rem(dp,2)
+    return z,x,c,t
+def dev(z,x,c,t):
+    return ((z*NX+x)*NC+c,t)
+
+def peers():
+    z,x,c,t=place()
+    zp=[dev(lax.rem(z+d,NZ),x,c,t) for d in range(1,NZ)]
+    return zp,dev(z,1-x,c,t),dev(z,x,c,1-t),dev(z,x,1-c,t)
+
+def greet():
+    zp,xp,yp,sp=peers()
+    bar=pltpu.get_barrier_semaphore()
+    for d in zp+[xp,yp,sp]:
+        pl.semaphore_signal(bar,inc=1,device_id=d,device_id_type=MESH)
+    pl.semaphore_wait(bar,6)
+
+def rcopy(src,dst,ssem,rsem,d):
+    return pltpu.make_async_remote_copy(src_ref=src,dst_ref=dst,send_sem=ssem,recv_sem=rsem,device_id=d,device_id_type=MESH)
+
+def gather_kernel(chunks,w_ref,g_ref,lsem,zs,zr,xs,xr,ys,yr,ss,sr):
+    z,x,c,t=place()
+    zp,xp,yp,sp=peers()
+    greet()
+    n=len(chunks)
+    def cols(i): return pl.ds(chunks[i][0],chunks[i][1])
+    def ca(i): return pl.ds(chunks[i][0],chunks[i][2])
+    def cb(i): return pl.ds(chunks[i][0]+chunks[i][2],chunks[i][1]-chunks[i][2])
+    def zcopies(i):
+        return [rcopy(w_ref.at[:,cols(i)],g_ref.at[t,z,x,c,:,cols(i)],zs.at[i,d],zr.at[i,d],zp[d]) for d in range(3)]
+    def first(i):
+        return [rcopy(g_ref.at[t,:,x,c,:,ca(i)],g_ref.at[t,:,x,c,:,ca(i)],xs.at[i,0],xr.at[i,0],xp),
+                rcopy(g_ref.at[t,:,x,c,:,cb(i)],g_ref.at[t,:,x,c,:,cb(i)],ys.at[i,0],yr.at[i,0],yp)]
+    def second(i):
+        return [rcopy(g_ref.at[t,:,:,c,:,ca(i)],g_ref.at[t,:,:,c,:,ca(i)],ys.at[i,1],yr.at[i,1],yp),
+                rcopy(g_ref.at[:,:,x,c,:,cb(i)],g_ref.at[:,:,x,c,:,cb(i)],xs.at[i,1],xr.at[i,1],xp)]
+    def sib(i):
+        return [rcopy(g_ref.at[:,:,:,c,:,cols(i)],g_ref.at[:,:,:,c,:,cols(i)],ss.at[i],sr.at[i],sp)]
+    locs=[pltpu.make_async_copy(w_ref.at[:,cols(i)],g_ref.at[t,z,x,c,:,cols(i)],lsem.at[i]) for i in range(n)]
+    Z=[zcopies(i) for i in range(n)]; A=[first(i) for i in range(n)]; B=[second(i) for i in range(n)]; S=[sib(i) for i in range(n)]
+    for i in range(n):
+        locs[i].start()
+        for q in Z[i]: q.start()
+    for step in range(n+3):
+        if step<n:
+            locs[step].wait()
+            for q in Z[step]: q.wait_recv()
+            for q in A[step]: q.start()
+        j=step-1
+        if 0<=j<n:
+            for q in A[j]: q.wait_recv()
+            for q in B[j]: q.start()
+        j=step-2
+        if 0<=j<n:
+            for q in B[j]: q.wait_recv()
+            for q in S[j]: q.start()
+    for i in range(n):
+        for q in Z[i]+A[i]+B[i]: q.wait_send()
+        for q in S[i]: q.wait()
+
+def gather(w,chunks,space=pl.ANY,cid=0):
+    n=len(chunks); DMA=pltpu.SemaphoreType.DMA
+    width=w.shape[1]
+    return pl.pallas_call(functools.partial(gather_kernel,chunks),
+        in_specs=[pl.BlockSpec(memory_space=space)],out_specs=pl.BlockSpec(memory_space=space),
+        out_shape=jax.ShapeDtypeStruct((NT,NZ,NX,NC,ROWS,width),BF),
+        scratch_shapes=[DMA((n,)),DMA((n,3)),DMA((n,3)),DMA((n,2)),DMA((n,2)),DMA((n,2)),DMA((n,2)),DMA((n,)),DMA((n,))],
+        compiler_params=pltpu.CompilerParams(collective_id=cid,has_side_effects=True,vmem_limit_bytes=60*2**20),name="gather")(w)
+
+def scatter_kernel(chunks,g_hbm,o_ref,g,rs,ra,rc,rb,rz,lsem,ss,sr,as_,ar,bs,br,zs,zr):
+    z,x,c,t=place()
+    zp,xp,yp,sp=peers()
+    n=len(chunks)
+    def cols(i): return pl.ds(chunks[i][0],chunks[i][1])
+    def ca(i): return pl.ds(chunks[i][0],chunks[i][2])
+    def cb(i): return pl.ds(chunks[i][0]+chunks[i][2],chunks[i][1]-chunks[i][2])
+    L=[pltpu.make_async_copy(g_hbm.at[:,:,:,:,:,cols(i)],g.at[:,:,:,:,:,cols(i)],lsem.at[i]) for i in range(n)]
+    for q in L: q.start()
+    greet()
+    S=[[rcopy(g.at[:,:,:,1-c,:,cols(i)],rs.at[:,:,:,:,cols(i)],ss.at[i],sr.at[i],sp)] for i in range(n)]
+    A=[[rcopy(g.at[:,:,1-x,c,:,ca(i)],ra.at[:,:,:,ca(i)],as_.at[i,0],ar.at[i,0],xp),
+        rcopy(g.at[1-t,:,:,c,:,cb(i)],rc.at[:,:,:,cb(i)],as_.at[i,1],ar.at[i,1],yp)] for i in range(n)]
+    B=[[rcopy(g.at[1-t,:,x,c,:,ca(i)],rb.at[:,:,ca(i)],bs.at[i,0],br.at[i,0],yp),
+        rcopy(g.at[t,:,1-x,c,:,cb(i)],rb.at[:,:,cb(i)],bs.at[i,1],br.at[i,1],xp)] for i in range(n)]
+    Zc=[[rcopy(g.at[t,lax.rem(z+d+1,NZ),x,c,:,cols(i)],rz.at[d,:,cols(i)],zs.at[i,d],zr.at[i,d],zp[d]) for d in range(3)] for i in range(n)]
+    def addS(i):
+        def body(k,_):
+            tt=lax.div(k,8); zz=lax.rem(lax.div(k,2),4); xx=lax.rem(k,2)
+            g[tt,zz,xx,c,:,cols(i)]=(g[tt,zz,xx,c,:,cols(i)].astype(F32)+rs[tt,zz,xx,:,cols(i)].astype(F32)).astype(BF)
+            return 0
+        lax.fori_loop(0,16,body,0)
+    def addA(i):
+        def body(k,_):
+            a=lax.div(k,4); b=lax.rem(k,4)
+            g[a,b,x,c,:,ca(i)]=(g[a,b,x,c,:,ca(i)].astype(F32)+ra[a,b,:,ca(i)].astype(F32)).astype(BF)
+            zz=lax.div(k,2); xx=lax.rem(k,2)
+            g[t,zz,xx,c,:,cb(i)]=(g[t,zz,xx,c,:,cb(i)].astype(F32)+rc[zz,xx,:,cb(i)].astype(F32)).astype(BF)
+            return 0
+        lax.fori_loop(0,8,body,0)
+    def addB(i):
+        def body(k,_):
+            g[t,k,x,c,:,cols(i)]=(g[t,k,x,c,:,cols(i)].astype(F32)+rb[k,:,cols(i)].astype(F32)).astype(BF)
+            return 0
+        lax.fori_loop(0,4,body,0)
+    def addZ(i):
+        acc=g[t,z,x,c,:,cols(i)].astype(F32)
+        for d in range(3): acc=acc+rz[d,:,cols(i)].astype(F32)
+        o_ref[:,cols(i)]=acc
+    for step in range(n+4):
+        if step<n:
+            L[step].wait()
+            for q in S[step]: q.start()
+        j=step-1
+        if 0<=j<n:
+            for q in S[j]: q.wait_recv()
+            addS(j)
+            for q in A[j]: q.start()
+        j=step-2
+        if 0<=j<n:
+            for q in A[j]: q.wait_recv()
+            addA(j)
+            for q in B[j]: q.start()
+        j=step-3
+        if 0<=j<n:
+            for q in B[j]: q.wait_recv()
+            addB(j)
+            for q in Zc[j]: q.start()
+        j=step-4
+        if 0<=j<n:
+            for q in Zc[j]: q.wait_recv()
+            addZ(j)
+    for i in range(n):
+        for q in S[i]+A[i]+B[i]+Zc[i]: q.wait_send()
+
+def scatter(g,chunks,cid=1):
+    n=len(chunks); DMA=pltpu.SemaphoreType.DMA
+    W=g.shape[-1]; V=lambda *s:pltpu.VMEM(s+(ROWS,W),BF)
+    return pl.pallas_call(functools.partial(scatter_kernel,chunks),
+        in_specs=[pl.BlockSpec(memory_space=pl.ANY)],out_specs=pl.BlockSpec(memory_space=pltpu.VMEM),
+        out_shape=jax.ShapeDtypeStruct((ROWS,W),F32),
+        scratch_shapes=[V(NT,NZ,NX,NC),V(NT,NZ,NX),V(NT,NZ),V(NZ,NX),V(NZ),V(3),
+          DMA((n,)),DMA((n,)),DMA((n,)),DMA((n,2)),DMA((n,2)),DMA((n,2)),DMA((n,2)),DMA((n,3)),DMA((n,3))],
+        compiler_params=pltpu.CompilerParams(collective_id=cid,has_side_effects=True,vmem_limit_bytes=62*2**20),name="scatter")(g)
+def mkchunks(ws):
+    out=[];s=0
+    for w in ws:
+        w*=128
+        out.append((s,w,(w//256)*128)); s+=w
+    return out
+
+CHUNKS=mkchunks([6,6,9,6,6,6])
+L=1024
+def dot(a,b,ca,cb):
+    return lax.dot_general(a,b,(((ca,),(cb,)),((),())),preferred_element_type=F32)
+def fwdT(bk, q_ref,k_ref,v_ref,bias_ref,o_ref,lse_ref):
+    lane=lax.broadcasted_iota(jnp.int32,(1,128),1)
+    qp=q_ref[...]; kp=k_ref[...]; vp=v_ref[...]
+    bias=bias_ref[...]
+    vT=vp.T
+    outs=[]
+    for h in range(2):
+        sel=(lane//64)==h
+        one=lane==(64*(1-h))
+        kh=jnp.where(sel,kp,jnp.where(one,bias.astype(BF),jnp.zeros_like(kp)))
+        qh=jnp.where(sel,qp*0.125,jnp.where(one,jnp.ones_like(qp),jnp.zeros_like(qp)))
+        oT=[]
+        for qi in range(L//bk):
+            sT=dot(kh,qh[qi*bk:(qi+1)*bk],1,1)
+            m=jnp.max(sT,axis=0,keepdims=True)
+            e=jnp.exp(sT-m)
+            l=jnp.sum(e,axis=0,keepdims=True)
+            p=(e*(1.0/l)).astype(BF)
+            oT.append(dot(vT[h*64:(h+1)*64],p,1,0))
+            lse_ref[0,h:h+1,qi*bk:(qi+1)*bk]=m+jnp.log(l)
+        outs.append(jnp.concatenate(oT,axis=1))
+    oT=jnp.concatenate(outs,axis=0)
+    o_ref[...]=oT.T.astype(BF)
+
+def call_fwd(body,b,q,k,v,bias):
+    return pl.pallas_call(functools.partial(body,b),grid=(6,),
+      in_specs=[pl.BlockSpec((L,128),lambda i:(0,i))]*3+[pl.BlockSpec((L,1),lambda i:(0,0))],
+      out_specs=[pl.BlockSpec((L,128),lambda i:(0,i)),pl.BlockSpec((1,2,L),lambda i:(i,0,0))],
+      out_shape=[jax.ShapeDtypeStruct((L,768),BF),jax.ShapeDtypeStruct((6,2,L),F32)],
+      compiler_params=pltpu.CompilerParams(vmem_limit_bytes=60*2**20),name=f"{body.__name__}_{b}")(q,k,v,bias)
+
+def bwdT(bq, q_ref,k_ref,v_ref,do_ref,bias_ref,lse_ref,dq_ref,dk_ref,dv_ref):
+    lane=lax.broadcasted_iota(jnp.int32,(1,128),1)
+    kp=k_ref[...]; vp=v_ref[...]
+    bias=bias_ref[...]
+    khs=[];vhs=[];kts=[]
+    for h in range(2):
+        sel=(lane//64)==h
+        one=lane==(64*(1-h))
+        khs.append(jnp.where(sel,kp,jnp.where(one,bias.astype(BF),jnp.zeros_like(kp))))
+        vhs.append(jnp.where(sel,vp,jnp.zeros_like(vp)))
+    kT=kp.T
+    dk=[None,None];dv=[None,None]
+    for qi in range(L//bq):
+        rows=pl.ds(qi*bq,bq)
+        qp=q_ref[rows,:]; dop=do_ref[rows,:]
+        dqT=[]
+        for h in range(2):
+            sel=(lane//64)==h
+            one=lane==(64*(1-h))
+            qh=jnp.where(sel,qp*0.125,jnp.where(one,jnp.ones_like(qp),jnp.zeros_like(qp)))
+            doh=jnp.where(sel,dop,jnp.zeros_like(dop))
+            qz=jnp.where(sel,qp*0.125,jnp.zeros_like(qp))
+            sT=dot(khs[h],qh,1,1)
+            p=jnp.exp(sT-lse_ref[0,h:h+1,qi*bq:(qi+1)*bq])
+            dp=dot(vhs[h],doh,1,1)
+            d=jnp.sum(p*dp,axis=0,keepdims=True)
+            ds=(p*(dp-d)).astype(BF)
+            pb=p.astype(BF)
+            a=dot(pb,doh,1,0); dv[h]=a if dv[h] is None else dv[h]+a
+            a=dot(ds,qz,1,0); dk[h]=a if dk[h] is None else dk[h]+a
+            dqT.append(dot(kT[h*64:(h+1)*64],ds,1,0))
+        dq_ref[rows,:]=(jnp.concatenate(dqT,axis=0).T*0.125)
+    dk_ref[...]=dk[0]+dk[1]
+    dv_ref[...]=dv[0]+dv[1]
+
+def call_bwd(body,b,q,k,v,do,bias,lse):
+    return pl.pallas_call(functools.partial(body,b),grid=(6,),
+      in_specs=[pl.BlockSpec((L,128),lambda i:(0,i))]*4+[pl.BlockSpec((L,1),lambda i:(0,0)),pl.BlockSpec((1,2,L),lambda i:(i,0,0))],
+      out_specs=[pl.BlockSpec((L,128),lambda i:(0,i))]*3,
+      out_shape=[jax.ShapeDtypeStruct((L,768),F32)]*3,
+      compiler_params=pltpu.CompilerParams(vmem_limit_bytes=60*2**20),name=f"{body.__name__}_{b}")(q,k,v,do,bias,lse)
+
+
+def ln_stats(v):
+    mean=jnp.mean(v,axis=-1,keepdims=True)
+    cen=v-mean
+    inv=lax.rsqrt(jnp.mean(cen*cen,axis=-1,keepdims=True)+EPSILON)
+    return cen*inv,inv
+
+def ln_back(gain,dy,xhat,inv):
+    gd=gain*dy
+    return (gd-jnp.mean(gd,axis=-1,keepdims=True)-xhat*jnp.mean(gd*xhat,axis=-1,keepdims=True))*inv
+
+def phi_cdf(u):
+    return 0.5*(1.0+lax.erf(u*(1.0/math.sqrt(2.0))))
+
+def pack_weights(qkv,out,up,down,w1,w2,b1,hv,lv):
+    t=lax.axis_index("tensor")
+    low=lambda a:a.astype(BF)
+    w2h=lax.dynamic_slice_in_dim(low(w2),t*PIECE,PIECE,1)
+    w1h=lax.dynamic_slice_in_dim(jnp.pad(low(w1),((0,8),(0,0))),t*256,256,1)
+    lanes=lambda a:jnp.pad(low(a),((0,0),(0,128-a.shape[1])))
+    vec=jnp.concatenate([lanes(lv),lanes(hv[:,0]),lanes(b1[None]),jnp.zeros((2,128),BF)],axis=0)
+    aux=jnp.concatenate([w2h,jnp.concatenate([w1h,vec],axis=1)],axis=0)
+    return jnp.concatenate([aux,low(qkv).reshape(ROWS,3*PIECE),low(out).T,low(up).reshape(ROWS,4*PIECE),low(down).transpose(2,0,1).reshape(ROWS,4*PIECE)],axis=1)
+
+def shards_fast(tokens,cotangent,segment_ids,timesteps,*params):
+    masters=params[:9];moments=params[9:18];averages=params[18:]
+    t=lax.axis_index("tensor")
+    g=gather(pack_weights(*masters),CHUNKS)
+    g=g.reshape(NT,16,ROWS,13*PIECE)
+    aux=g[...,:PIECE]
+    both=lambda a:jnp.concatenate([a[0],a[1]],axis=-1)
+    w2=both(aux[:,:,:32].reshape(NT,512,PIECE))
+    w1=both(aux[:,:,32:,:256].reshape(NT,256,256))
+    vec=aux[:,:,32:,256:].astype(F32)
+    lv=vec[0,:,0:7,0:48].transpose(1,0,2).reshape(7,D)
+    hv=vec[:,:,7:13,0:24].transpose(2,0,1,3).reshape(6,D)
+    b1=vec[0,:,13,0:32].reshape(1,512)
+    wide=g.reshape(NT,D,13*PIECE)
+    w_qkv=wide[...,PIECE:4*PIECE].reshape(NT,D,3,PIECE)
+    w_outT=wide[...,4*PIECE:5*PIECE]
+    w_up=wide[...,5*PIECE:9*PIECE]
+    w_downT=wide[...,9*PIECE:]
+
+    seg=lax.dynamic_slice_in_dim(segment_ids[0],t*512,L,0)
+    own=(seg==t)[:,None]
+    tok=lax.dynamic_slice_in_dim(tokens,t*512,L,0).astype(F32)
+    dy=jnp.where(own,lax.dynamic_slice_in_dim(cotangent,t*512,L,0).astype(F32),0.0)
+    step=lax.dynamic_slice_in_dim(timesteps,t,1,1)[0]
+    feat=time_features(step,TD).astype(BF)
+    featp=jnp.pad(feat.reshape(16,8),((0,0),(0,8))).reshape(1,256)
+    inner=dot(featp,w1,1,0)+b1
+    sig=jax.nn.sigmoid(inner)
+    act=(inner*sig).astype(BF)
+    temb=dot(act,w2,1,0)+lv[6:7]
+    h0=tok+temb
+    hb=h0.astype(BF)
+    proj=jnp.einsum("pd,tdce->pcte",hb,w_qkv,preferred_element_type=F32).reshape(L,3,D)
+    q=(proj[:,0]+hv[0]).astype(BF); k=proj[:,1].astype(BF); v=(proj[:,2]+hv[1]).astype(BF)
+    bias=jnp.where(own,0.0,-1e30).astype(F32)
+    o,lse=call_fwd(fwdT,512,q,k,v,bias)
+    attn=jnp.einsum("pte,tfe->pf",o.reshape(L,NT,PIECE),w_outT,preferred_element_type=F32)+lv[0]
+    x1,inv1=ln_stats(h0+attn)
+    a=x1*lv[1]+lv[2]
+    ab=a.astype(BF)
+    bup=hv[2:].reshape(4,NT,PIECE).transpose(1,0,2).reshape(NT,4*PIECE)
+    u=jnp.einsum("pd,tdj->ptj",ab,w_up,preferred_element_type=F32)+bup
+    cdf=phi_cdf(u)
+    hid=(u*cdf).astype(BF)
+    mlp=jnp.einsum("ptj,tfj->pf",hid,w_downT,preferred_element_type=F32)+lv[3]
+    x2,inv2=ln_stats(a+mlp)
+    out_win=(x2*lv[4]+lv[5]).astype(BF)
+    g_gain2=jnp.sum(dy*x2,0); g_shift2=jnp.sum(dy,0)
+    dr2=ln_back(lv[4],dy,x2,inv2)
+    g_bdown=jnp.sum(dr2,0)
+    dmb=dr2.astype(BF)
+    g_down=jnp.einsum("pf,ptj->tfj",dmb,hid,preferred_element_type=F32)
+    dhid=jnp.einsum("pf,tfj->ptj",dmb,w_downT,preferred_element_type=F32)
+    du=dhid*(cdf+u*jnp.exp(-0.5*u*u)*(1.0/math.sqrt(2*math.pi)))
+    g_bup=jnp.sum(du,0)
+    dub=du.astype(BF)
+    g_up=jnp.einsum("pd,ptj->tdj",ab,dub,preferred_element_type=F32)
+    da=jnp.einsum("ptj,tdj->pd",dub,w_up,preferred_element_type=F32)+dr2
+    g_gain1=jnp.sum(da*x1,0); g_shift1=jnp.sum(da,0)
+    dr1=ln_back(lv[1],da,x1,inv1)
+    g_bo=jnp.sum(dr1,0)
+    drb=dr1.astype(BF)
+    g_out=jnp.einsum("pf,pte->tfe",drb,o.reshape(L,NT,PIECE),preferred_element_type=F32)
+    dob=jnp.einsum("pf,tfe->pte",drb,w_outT,preferred_element_type=F32).astype(BF).reshape(L,D)
+    dq,dk,dv=call_bwd(bwdT,512,q,k,v,dob,bias,lse)
+    g_bq=jnp.sum(dq,0); g_bv=jnp.sum(dv,0)
+    dqkv=jnp.stack([dq,dk,dv],axis=1).astype(BF).reshape(L,3,NT,PIECE)
+    g_qkv=jnp.einsum("pd,pcte->tdce",hb,dqkv,preferred_element_type=F32)
+    dh0=jnp.einsum("pcte,tdce->pd",dqkv,w_qkv,preferred_element_type=F32)+dr1
+    in_win=dh0.astype(BF)
+    dtemb=jnp.sum(dh0,0,keepdims=True)
+    dtb=dtemb.astype(BF)
+    g_w2=dot(act,dtb,0,0)
+    dinner=dot(dtb,w2,1,1)*(sig*(1.0+inner*(1.0-sig)))
+    g_w1=dot(featp,dinner.astype(BF),0,0)
+    g_lv=jnp.stack([g_bo,g_gain1,g_shift1,g_bdown,g_gain2,g_shift2,dtemb[0]],0)
+    g_bup=g_bup.reshape(NT,4,PIECE).transpose(1,0,2).reshape(4,D)
+    g_hv=jnp.concatenate([g_bq[None],g_bv[None],g_bup],0)
+    low=lambda a:a.astype(BF)
+    padl=lambda a:jnp.pad(low(a),((0,0),)*3+((0,128-a.shape[-1]),))
+    lvp=jnp.broadcast_to(padl(g_lv.reshape(7,16,48).transpose(1,0,2)[None]),(NT,16,7,128))
+    hvp=padl(g_hv.reshape(6,NT,16,24).transpose(1,2,0,3))
+    b1p=jnp.broadcast_to(padl(dinner.reshape(1,16,1,32)),(NT,16,1,128))
+    vecp=jnp.concatenate([lvp,hvp,b1p,jnp.zeros((NT,16,2,128),BF)],axis=2)
+    split=lambda a,r,w:low(a).reshape(16,r,NT,w).transpose(2,0,1,3)
+    auxg=jnp.concatenate([split(g_w2,32,PIECE),jnp.concatenate([split(g_w1,16,256),vecp],axis=3)],axis=2)
+    slab=lambda a:low(a).reshape(NT,16,ROWS,-1)
+    big=jnp.concatenate([auxg,slab(g_qkv),slab(g_out),slab(g_up),slab(g_down)],axis=3).reshape(NT,NZ,NX,NC,ROWS,13*PIECE)
+    red=scatter(big,CHUNKS)
+    swap=lambda a:lax.ppermute(a,"tensor",[(0,1),(1,0)])
+    aux_mine=red[:,:PIECE].astype(BF)
+    aux_peer=swap(aux_mine)
+    aux0=jnp.where(t==0,aux_mine,aux_peer).astype(F32); aux1=jnp.where(t==0,aux_peer,aux_mine).astype(F32)
+    r_qkv=red[:,PIECE:4*PIECE].reshape(ROWS,3,PIECE)
+    r_out=red[:,4*PIECE:5*PIECE].T
+    r_up=red[:,5*PIECE:9*PIECE].reshape(ROWS,4,PIECE)
+    r_down=red[:,9*PIECE:].reshape(ROWS,4,PIECE).transpose(1,2,0)
+    r_w2=jnp.concatenate([aux0[:32],aux1[:32]],axis=1)
+    r_w1=jnp.concatenate([aux0[32:40,:256],aux1[32:40,:256]],axis=1)
+    r_lv=aux0[32:39,256:304]
+    r_b1=aux0[45,256:288]
+    r_hv=jnp.where(t==0,aux0,aux1)[39:45,256:280].reshape(6,1,24)
+    grads=(r_qkv,r_out,r_up,r_down,r_w1,r_w2,r_b1,r_hv,r_lv)
+    sq=lambda a:jnp.sum(a*a)
+    squares=sum(sq(grads[i]) for i in (0,1,2,3,7))+0.5*sum(sq(grads[i]) for i in (4,5,6,8))
+    norm=jnp.sqrt(lax.psum(squares,("dp","tensor")))
+    factor=1.0/jnp.maximum(norm,1.0)
+    rate=4.0*math.sqrt(MPARAMS/D)
+    new=[advance(m,v_,a_,g_,factor,rate) for m,v_,a_,g_ in zip(masters,moments,averages,grads)]
+
+    def whole(win):
+        peer=swap(win)
+        lo=jnp.where(t==0,win,peer); hi=jnp.where(t==0,peer,win)
+        mid=jnp.where((segment_ids[0,512:1024]==0)[:,None],lo[512:],hi[:512])
+        return jnp.concatenate([lo[:512],mid,hi[512:]],axis=0)
+    return (whole(out_win),whole(in_win),norm)+tuple(n[0] for n in new)+tuple(n[1] for n in new)+tuple(n[2] for n in new)
+
+
 def solution(mesh):
+    fast=dict(mesh.shape)=={'dp':16,'tensor':2}
     return jax.shard_map(
-        shards,
+        shards_fast if fast else shards_any,
         mesh=mesh,
         in_specs=(
             P("dp", None),

time: 1390 us -> 658 us (0.47)
  waiting for transfers between devices: 646 us -> 0.01 us
  Pallas kernels: 0 us -> 243 us
  matrix products: 246 us -> 99.8 us
  blocking collectives: 229 us -> 85.8 us
  other arithmetic: 124 us -> 78.6 us
  local copies, waits for them, and re-layouts: 90.9 us -> 127 us
  loops' own time: 21.4 us -> 0 us
  between operations: 25 us -> 9.6 us
    reduce_scatter x6 -> x0, waiting for transfers between devices: 347 us -> none  [the longest x1 77.2 us: shards(): lax.psum_scatter(grad_down, 'dp', scatter_dimension=2, tiled=True)]
    psum x4 -> x0, waiting for transfers between devices: 254 us -> none  [the longest x1 68.7 us: shards(): lax.psum(back_a_part.astype(jnp.bfloat16), 'tensor').astype(jnp.float32)]
    pallas_call x0 -> x4, Pallas kernels: none -> 243 us  [the longest x1 88.1 us: scatter(): pl.pallas_call(functools.partial(scatter_kernel, chunks), in_specs=[pl.Bl...]
    dot_general x145 -> x15, matrix products: 246 us -> 99.8 us  [the longest x1 13.7 us: shards_fast(): dhid = jnp.einsum('pf,tfj->ptj', dmb, w_downT, preferred_element_type=F32)]
    all_gather x5 -> x0, blocking collectives: 102 us -> none  [the longest x1 23.1 us: shards(): lax.all_gather(layer_vectors.astype(jnp.bfloat16), 'dp', axis=1, tiled=True)]
    unnamed x2 -> x0, blocking collectives: 87.6 us -> none
    psum x1, blocking collectives: 39.6 us -> 85.8 us  [shards_fast(): norm = jnp.sqrt(lax.psum(squares, ('dp', 'tensor')))]
    all_gather x3 -> x0, waiting for transfers between devices: 45.2 us -> none  [the longest x1 37.8 us: shards(): lax.all_gather(up_weight.astype(jnp.bfloat16), 'dp', axis=0, tiled=True)]
  transfers between devices with their start and end apart: 14 -> 3, of which waited for: 12 -> 0; matrix products, arithmetic and copies ran while one was open for 9% -> 5% of each run, Pallas kernels for 0% -> 0%
where the time goes in v1:
time: 658 us; the launch traced here: 646 us
  Pallas kernels  243 us (37%)
  local copies, waits for them, and re-layouts  127 us (19%)
  matrix products  99.8 us (15%)
  blocking collectives  85.8 us (13%)
  other arithmetic  78.6 us (12%)
  between operations  9.6 us (1%)
    pallas_call x1, Pallas kernels, scatter(): pl.pallas_call(functools.partial(scatter_kernel, chunks), in_specs=[pl.Bl...  88.1 us
    pallas_call x1, Pallas kernels, gather(): pl.pallas_call(functools.partial(gather_kernel, chunks), in_specs=[pl.Blo...  86.9 us
    psum x1, blocking collectives, shards_fast(): norm = jnp.sqrt(lax.psum(squares, ('dp', 'tensor')))  85.8 us
    pallas_call x1, Pallas kernels, call_bwd(): pl.pallas_call(functools.partial(body, b), grid=(6,), in_specs=[pl.BlockS...  41.7 us
    pallas_call x1, Pallas kernels, call_fwd(): pl.pallas_call(functools.partial(body, b), grid=(6,), in_specs=[pl.BlockS...  26.3 us
    unnamed x118, local copies, waits for them, and re-layouts  25.7 us
    transpose x1, local copies, waits for them, and re-layouts, shards_fast(): jnp.einsum('pd,tdce->pcte', hb, w_qkv, preferred_element_type=F32)  14.8 us
    add x9, other arithmetic, advance(): smoothed = AVERAGE_DECAY * average + (1.0 - AVERAGE_DECAY) * fresh_master  14.5 us
  transfers between devices with their start and end apart: 3, of which 0 were waited for; matrix products, arithmetic and copies ran while one was open for 5% of the time, Pallas kernels for 0%

profile of v1, /device:TPU:0, one launch (start us, length us, event | category | flops | bytes accessed | tf_op | source)
XLA Modules:
  0.0 645.6 jit_solution(3579780104388825025)
XLA Ops:
  9.1 86.9 %gather.1 = bf16[2,4,2,2,48,4992]{5,4,3,2,1,0:T(8,128)(2,1)} custom-call(bf16[48,4992]{1,0:T(8,128)(2,1)} %copy-done.14), custom_call_target="tpu_custom_call" | custom-call | tf_op jit(solution)/shard_map/gather/pallas_call | solution.py:440
  109.2 3.6 copy.92
  114.8 9.9 %convolution_bitcast_fusion = f32[1024,3,2,384]{0,3,1,2:T(8,128)} fusion(bf16[2,768,3,384]{1,3,2,0:T(8,128)(2,1)} %bitcast.218, f32[768]{0:T(1024)S(1)} %add.283, bf16[1536,768]{1,0:T(8,128)(2,1)} %param.31, s32[]{:T(128)S(6)} %select_n.70), kind=kOutput, calls=%fused_computation.22 | convolution fusion | flops 3626237952 | bytes 14552068 | tf_op jit(solution)/shard_map/pd,tdce->pcte/dot_general | solution.py:660
  124.7 14.8 %copy.93 = f32[1024,3,2,384]{3,2,0,1:T(2,128)} copy(f32[1024,3,2,384]{0,3,1,2:T(8,128)} %convolution_bitcast_fusion) | data formatting | bytes 18874368 | tf_op jit(solution)/shard_map/pd,tdce->pcte/transpose | solution.py:660
  139.5 13.0 %reshape.372 = f32[1024,3,768]{2,0,1:T(8,128)} reshape(f32[1024,3,2,384]{3,2,0,1:T(2,128)} %copy.93) | data formatting | bytes 18874368 | tf_op jit(solution)/shard_map/reshape | solution.py:660
  152.7 3.2 fusion.37.k_ref
  156.9 5.0 fusion.15
  161.9 26.3 %fwdT_512.1 = (bf16[1024,768]{1,0:T(8,128)(2,1)}, f32[6,2,1024]{2,1,0:T(2,128)}) custom-call(bf16[1024,768]{1,0:T(8,128)(2,1)} %get-tuple-element.150.q_ref, bf16[1024,768]{1,0:T(8,128)(2,1)} %fusion.37.k_ref, bf16[1024,768]{1,0:T(8,128)(2,1)} %get-tuple-element.149.v_ref, f32[1024,1]{1,0:T(8,128)} %copy.94.bias_ref), custom_call_target="tpu_custom_call" | custom-call | tf_op jit(solution)/shard_map/fwdT_512/pallas_call | solution.py:556
  188.2 2.8 copy.139
  191.1 3.9 fusion.118
  196.2 10.8 %multiply_convert_fusion = (bf16[1024,2,1536]{2,0,1:T(8,128)(2,1)S(1)}, f32[1024,2,1536]{2,0,1:T(8,128)}) fusion(f32[2,1536]{1,0:T(2,128)S(1)} %bitcast.237, bf16[2,768,4992]{2,1,0:T(8,128)(2,1)} %bitcast.207, f32[1024,768]{1,0:T(8,128)S(1)} %get-tuple-element.184, f32[768]{0:T(1024)S(1)} %add.297, f32[768]{0:T(1024)S(1)} %mul.450, ...), kind=kOutput, calls=%fused_computation.6 | convolution fusion | flops 4854644736 | bytes 26765312 | tf_op jit(solution)/shard_map/pd,tdj->ptj/dot_general | solution.py:669
  207.0 11.0 %fusion.119 = (f32[1024]{0:T(1024)S(1)}, f32[1024,768]{1,0:T(8,128)S(1)}) fusion(f32[768]{0:T(1024)S(1)} %add.305, bf16[1024,2,1536]{2,0,1:T(8,128)(2,1)S(1)} %get-tuple-element.185, bf16[2,768,4992]{2,1,0:T(8,128)(2,1)} %bitcast.208, f32[768]{0:T(1024)S(1)} %add.297, f32[768]{0:T(1024)S(1)} %mul.450, f32[1024]{0:T(1024)S(1)} %add_rsqrt_fusion.1, ...), kind=kOutput, calls=%fused_computation.249 | convolution fusion | flops 4837342208 | bytes 17323008 | tf_op jit(solution)/shard_map/ptj,tfj->pf/dot_general | solution.py:672
  218.9 3.5 multiply_reduce_fusion
  222.4 4.8 fusion.106
  227.2 13.7 %fusion.120 = (bf16[2,1536]{1,0:T(2,128)(2,1)}, bf16[1024,2,1536]{2,0,1:T(8,128)(2,1)S(1)}) fusion(f32[1024,2,1536]{2,0,1:T(8,128)} %get-tuple-element.186, f32[2,1536]{1,0:T(2,128)S(1)} %bitcast.238, bf16[2,768,4992]{2,1,0:T(8,128)(2,1)} %bitcast.209, f32[1024,768]{1,0:T(8,128)S(1)} %get-tuple-element.142), kind=kOutput, calls=%fused_computation.250 | convolution fusion | flops 4870370304 | bytes 26757120 | tf_op jit(solution)/shard_map/pf,tfj->ptj/dot_general | solution.py:680
  240.9 7.3 %convolution_convert_fusion.1 = bf16[2,1536,768]{1,2,0:T(8,128)(2,1)} fusion(bf16[1024,2,1536]{2,0,1:T(8,128)(2,1)S(1)} %get-tuple-element.192, f32[1024,768]{1,0:T(8,128)S(1)} %copy-done.1, f32[768]{0:T(1024)S(1)} %add.297, f32[768]{0:T(1024)S(1)} %mul.450, f32[1024]{0:T(1024)S(1)} %add_rsqrt_fusion.1, f32[1024]{0:T(1024)S(1)} %broadcast_multiply_fusion.5), kind=kOutput, calls=%fused_computation.11 | convolution fusion | flops 4838129664 | bytes 14170112 | tf_op jit(solution)/shard_map/pd,ptj->tdj/dot_general | solution.py:684
  248.2 8.9 %multiply_reduce_fusion.1 = (bf16[768]{0:T(1024)(128)(2,1)}, f32[1024]{0:T(1024)S(1)}, f32[1024]{0:T(1024)S(1)}, bf16[768]{0:T(1024)(128)(2,1)}, f32[1024,768]{1,0:T(8,128)S(1)}) fusion(f32[1024,768]{1,0:T(8,128)S(1)} %copy-done.1, f32[1024]{0:T(1024)S(1)} %add_rsqrt_fusion.1, f32[1024]{0:T(1024)S(1)} %broadcast_multiply_fusion.5, f32[768]{0:T(1024)S(1)} %mul.450, ...), kind=kOutput, calls=%fused_computation.37 | convolution fusion | flops 4839698432 | bytes 20469760 | tf_op jit(solution)/shard_map/ptj,tdj->pd/dot_general | solution.py:685
  258.9 3.6 convolution_convert_fusion.2
  264.1 41.7 %bwdT_512.1 = (f32[1024,768]{1,0:T(8,128)}, f32[1024,768]{1,0:T(8,128)}, f32[1024,768]{1,0:T(8,128)}) custom-call(bf16[1024,768]{1,0:T(8,128)(2,1)} %get-tuple-element.150.q_ref, bf16[1024,768]{1,0:T(8,128)(2,1)} %fusion.37.k_ref, bf16[1024,768]{1,0:T(8,128)(2,1)} %get-tuple-element.149.v_ref, bf16[1024,768]{1,0:T(8,128)(2,1)} %copy.134.do_ref, ...), custom_call_target="tpu_custom_call" | custom-call | tf_op jit(solution)/shard_map/bwdT_512/pallas_call | solution.py:598
  305.8 3.8 fusion.110
  313.1 4.9 fusion.111
  318.0 3.4 stack.37
  324.1 6.9 %convert_bitcast_fusion = bf16[2,768,3,384]{1,3,0,2:T(8,128)(2,1)S(1)} fusion(bf16[1024,3,2,384]{3,0,2,1:T(8,128)(2,1)} %copy_dynamic-update-slice_fusion, f32[768]{0:T(1024)S(1)} %copy-done.41, bf16[1536,768]{1,0:T(8,128)(2,1)S(1)} %copy-done.43, s32[]{:T(128)S(6)} %select_n.70), kind=kOutput, calls=%fused_computation.21 | convolution fusion | flops 3628007424 | bytes 9834500 | tf_op jit(solution)/shard_map/pd,pcte->tdce/dot_general | solution.py:695
  331.1 6.4 fusion.112
  338.8 4.9 fusion.46
  343.7 9.5 %convolution_convert_fusion = bf16[2,1536,768]{1,2,0:T(8,128)(2,1)} fusion(bf16[1024,2,1536]{2,0,1:T(8,128)(2,1)} %copy-done.45, f32[1024,768]{1,0:T(8,128)S(1)} %copy-done.8), kind=kOutput, calls=%fused_computation.10 | convolution fusion | flops 4834983936 | bytes 14155776 | tf_op jit(solution)/shard_map/pf,ptj->tfj/dot_general | solution.py:679
  353.2 5.7 copy.109
  358.9 7.9 %concatenate.91 = bf16[2,4,2,2,48,1152]{5,4,3,2,1,0:T(8,128)(2,1)S(1)} reshape(bf16[2,768,3,384]{3,2,1,0:T(4,128)(2,1)} %copy.109) | data formatting | bytes 7077888 | tf_op jit(solution)/shard_map/concatenate | solution.py:715
  399.3 5.9 maximum_maximum_fusion
  412.5 5.2 constant_dynamic-update-slice_fusion.13
  420.3 88.1 %scatter.1 = f32[48,4992]{1,0:T(8,128)} custom-call(bf16[2,4,2,2,48,4992]{5,4,3,2,1,0:T(8,128)(2,1)} %constant_dynamic-update-slice_fusion.12.g_hbm), custom_call_target="tpu_custom_call" | custom-call | tf_op jit(solution)/shard_map/scatter/pallas_call | solution.py:514
  527.4 85.8 %psum.7 = f32[]{:T(128)} all-reduce(f32[]{:T(128)S(6)} %add.324), channel_id=1, replica_groups=mesh['dp'=16,'tensor'=2] {'dp','tensor'}, use_global_device_ids=true, to_apply=%region_27.28 | all-reduce | flops 1 | bytes 8 | tf_op jit(solution)/shard_map/psum | solution.py:733
  (260 shorter events, 122.8 us)
Async XLA Ops:
  7.3 88.7 %copy-start.42 = (bf16[2,128]{1,0:T(2,128)(2,1)}, bf16[2,128]{1,0:T(2,128)(2,1)S(1)}, u32[]{:S(2)}) copy-start(bf16[2,128]{1,0:T(2,128)(2,1)S(1)} %broadcast_in_dim.43) | copy-start | bytes 1540
  96.0 5.4 copy-start.32
  96.0 6.6 %copy-start.44 = (s32[1,2]{1,0:T(1,128)S(1)}, s32[1,2]{1,0:T(1,128)}, u32[]{:S(2)}) copy-start(s32[1,2]{1,0:T(1,128)} %param.34) | copy-start | bytes 28
  114.8 76.3 %copy-start.40 = (f32[768]{0:T(1024)}, f32[768]{0:T(1024)S(1)}, u32[]{:S(2)}) copy-start(f32[768]{0:T(1024)S(1)} %add.283) | copy-start | bytes 9220
  139.5 13.0 %copy-start.21 = (f32[1,2,16,24]{3,2,1,0:T(8,128)S(1)}, f32[1,2,16,24]{3,2,1,0:T(8,128)}, u32[]{:S(2)}) copy-start(f32[1,2,16,24]{3,2,1,0:T(8,128)} %get-tuple-element.172) | copy-start | bytes 9220
  161.9 29.1 %copy-start.29 = (f32[1,16,48]{2,1,0:T(8,128)S(1)}, f32[1,16,48]{2,1,0:T(8,128)}, u32[]{:S(2)}) copy-start(f32[1,16,48]{2,1,0:T(8,128)} %get-tuple-element.180) | copy-start | bytes 9220
  195.0 12.0 %copy-start = (f32[1024,768]{1,0:T(8,128)}, f32[1024,768]{1,0:T(8,128)S(1)}, u32[]{:S(2)}) copy-start(f32[1024,768]{1,0:T(8,128)S(1)} %get-tuple-element.184) | copy-start | bytes 9437188
  207.0 11.0 %copy-start.45 = (bf16[1024,2,1536]{2,0,1:T(8,128)(2,1)}, bf16[1024,2,1536]{2,0,1:T(8,128)(2,1)S(1)}, u32[]{:S(2)}) copy-start(bf16[1024,2,1536]{2,0,1:T(8,128)(2,1)S(1)} %get-tuple-element.185) | copy-start | bytes 18874372
  227.2 21.0 %copy-start.7 = (f32[1024,768]{1,0:T(8,128)}, f32[1024,768]{1,0:T(8,128)S(1)}, u32[]{:S(2)}) copy-start(f32[1024,768]{1,0:T(8,128)S(1)} %get-tuple-element.142) | copy-start | bytes 9437188
  227.2 13.7 %copy-start.1 = (f32[1024,768]{1,0:T(8,128)S(1)}, f32[1024,768]{1,0:T(8,128)}, u32[]{:S(2)}) copy-start(f32[1024,768]{1,0:T(8,128)} %copy-done) | copy-start | bytes 9437188
  324.1 6.9 %copy-start.5 = (bf16[2,768,1152]{1,2,0:T(8,128)(2,1)S(1)}, bf16[2,768,1152]{1,2,0:T(8,128)(2,1)}, u32[]{:S(2)}) copy-start(bf16[2,768,1152]{1,2,0:T(8,128)(2,1)} %copy.92) | copy-start | bytes 10616836
  324.1 6.9 %copy-start.10 = (f32[1024,768]{1,0:T(8,128)S(1)}, f32[1024,768]{1,0:T(8,128)}, u32[]{:S(2)}) copy-start(f32[1024,768]{1,0:T(8,128)} %copy-done.9) | copy-start | bytes 9437188
  324.1 6.9 %copy-start.15 = (bf16[1024,3,2,384]{3,0,2,1:T(8,128)(2,1)S(1)}, bf16[1024,3,2,384]{3,0,2,1:T(8,128)(2,1)}, u32[]{:S(2)}) copy-start(bf16[1024,3,2,384]{3,0,2,1:T(8,128)(2,1)} %copy_dynamic-update-slice_fusion) | copy-start | bytes 14155780
  331.1 7.0 %copy-start.23 = (bf16[16,16]{1,0:T(8,128)(2,1)S(1)}, bf16[16,16]{1,0:T(8,128)(2,1)}, u32[]{:S(2)}) copy-start(bf16[16,16]{1,0:T(8,128)(2,1)} %copy-done.22) | copy-start | bytes 1540
  358.9 8.0 %copy-start.37 = (f32[512]{0:T(512)S(1)}, f32[512]{0:T(512)}, u32[]{:S(2)}) copy-start(f32[512]{0:T(512)} %get-tuple-element.137) | copy-start | bytes 6148
  366.9 5.2 copy-start.31
  412.5 5.2 slice-start
  412.5 5.2 slice-start.1
  420.3 91.2 %copy-start.3 = (bf16[1024,768]{1,0:T(8,128)(2,1)S(1)}, bf16[1024,768]{1,0:T(8,128)(2,1)}, u32[]{:S(2)}) copy-start(bf16[1024,768]{1,0:T(8,128)(2,1)} %get-tuple-element.151) | copy-start | bytes 4718596
  420.3 195.4 %copy-start.35 = (f32[7,48]{1,0:T(8,128)S(1)}, f32[7,48]{1,0:T(8,128)}, u32[]{:S(2)}) copy-start(f32[7,48]{1,0:T(8,128)} %param.43) | copy-start | bytes 4036
  420.3 196.7 %copy-start.20 = (f32[8,512]{1,0:T(8,128)S(1)}, f32[8,512]{1,0:T(8,128)}, u32[]{:S(2)}) copy-start(f32[8,512]{1,0:T(8,128)} %param.39) | copy-start | bytes 49156
  420.3 196.7 %copy-start.34 = (f32[8,512]{1,0:T(8,128)S(1)}, f32[8,512]{1,0:T(8,128)}, u32[]{:S(2)}) copy-start(f32[8,512]{1,0:T(8,128)} %param.57) | copy-start | bytes 49156
  420.3 198.1 %copy-start.16 = (f32[384,48]{0,1:T(8,128)S(1)}, f32[384,48]{0,1:T(8,128)}, u32[]{:S(2)}) copy-start(f32[384,48]{0,1:T(8,128)} %param.36) | copy-start | bytes 221188
  420.3 198.0 %copy-start.18 = (f32[384,48]{0,1:T(8,128)S(1)}, f32[384,48]{0,1:T(8,128)}, u32[]{:S(2)}) copy-start(f32[384,48]{0,1:T(8,128)} %param.54) | copy-start | bytes 221188
  420.3 198.0 %copy-start.19 = (f32[384,48]{0,1:T(8,128)S(1)}, f32[384,48]{0,1:T(8,128)}, u32[]{:S(2)}) copy-start(f32[384,48]{0,1:T(8,128)} %param.45) | copy-start | bytes 221188
  508.4 111.5 %copy-start.13 = (f32[48,3,384]{2,0,1:T(8,128)S(1)}, f32[48,3,384]{2,0,1:T(8,128)}, u32[]{:S(2)}) copy-start(f32[48,3,384]{2,0,1:T(8,128)} %param.35) | copy-start | bytes 663556
  508.4 114.5 %copy-start.2 = (f32[48,4992]{1,0:T(8,128)S(1)}, f32[48,4992]{1,0:T(8,128)}, u32[]{:S(2)}) copy-start(f32[48,4992]{1,0:T(8,128)} %scatter.1) | copy-start | bytes 2875396
  509.4 9.5 %collective-permute-start.2 = (bf16[48,384]{1,0:T(8,128)(2,1)S(1)}, bf16[48,384]{1,0:T(8,128)(2,1)S(1)}, u32[]{:S(2)}, u32[]{:S(2)}) collective-permute-start(bf16[48,384]{1,0:T(8,128)(2,1)S(1)} %slice.318), channel_id=1, source_target_pairs={{0,1},{1,0},{2,3},{3,2},{4,5},{5,4},{6,7},{7,6},{8,9},{9,8},{10,11... | collective-permute-start | bytes 110600 | tf_op jit(solution)/shard_map/ppermute | solution.py:717
  509.4 127.7 %collective-permute-start.1 = (bf16[1024,768]{1,0:T(8,128)(2,1)}, bf16[1024,768]{1,0:T(8,128)(2,1)}, u32[]{:S(2)}, u32[]{:S(2)}) collective-permute-start(bf16[1024,768]{1,0:T(8,128)(2,1)} %get-tuple-element.157), channel_id=1, source_target_pairs={{0,1},{1,0},{2,3},{3,2},{4,5},{5,4},{6,7},{7,6},{8,9},{9,8},{10,11... | collective-permute-start | bytes 4718600 | tf_op jit(solution)/shard_map/ppermute | solution.py:717
  511.4 127.6 %collective-permute-start = (bf16[1024,768]{1,0:T(8,128)(2,1)S(1)}, bf16[1024,768]{1,0:T(8,128)(2,1)}, u32[]{:S(2)}, u32[]{:S(2)}) collective-permute-start(bf16[1024,768]{1,0:T(8,128)(2,1)S(1)} %copy-done.3), channel_id=1, source_target_pairs={{0,1},{1,0},{2,3},{3,2},{4,5},{5,4},{6,7},{7,6},{8,9},{9,8},{10,11... | collective-permute-start | bytes 4718600 | tf_op jit(solution)/shard_map/ppermute | solution.py:717
  623.8 11.2 %copy-start.12 = (f32[48,1536]{1,0:T(8,128)S(1)}, f32[48,1536]{1,0:T(8,128)}, u32[]{:S(2)}) copy-start(f32[48,1536]{1,0:T(8,128)} %get-tuple-element.168) | copy-start | bytes 884740
  627.9 9.3 %copy-start.11 = (bf16[1024,768]{1,0:T(8,128)(2,1)S(1)}, bf16[1024,768]{1,0:T(8,128)(2,1)}, u32[]{:S(2)}) copy-start(bf16[1024,768]{1,0:T(8,128)(2,1)} %get-tuple-element.157) | copy-start | bytes 4718596
  (19 other events, 37.5 us)

commit v2 on v1

--- a/solution.py
+++ b/solution.py
@@ -625,70 +625,248 @@
     aux=jnp.concatenate([w2h,jnp.concatenate([w1h,vec],axis=1)],axis=0)
     return jnp.concatenate([aux,low(qkv).reshape(ROWS,3*PIECE),low(out).T,low(up).reshape(ROWS,4*PIECE),low(down).transpose(2,0,1).reshape(ROWS,4*PIECE)],axis=1)
 
+WIDE=13*PIECE
+RB=256
+def spread(blocks,w,tiles):
+    lane=lax.broadcasted_iota(jnp.int32,(16,128),1)
+    acc=[jnp.zeros((16,128),F32) for _ in range(tiles+1)]
+    for n,b in enumerate(blocks):
+        tile,s=divmod(n*w,128)
+        wide=jnp.concatenate([jnp.where(lane<w,b,0.0),jnp.zeros((16,128),F32)],axis=1)
+        if s: wide=pltpu.roll(wide,s,1)
+        acc[tile]=acc[tile]+wide[:,:128]
+        acc[tile+1]=acc[tile+1]+wide[:,128:]
+    return jnp.concatenate(acc[:tiles],axis=1)
+
+def attend_pair(q_ref,k_ref,v_ref,o_ref,lse_ref,bias_ref,i,bq=512):
+    lane=lax.broadcasted_iota(jnp.int32,(1,128),1)
+    cs=pl.ds(pl.multiple_of(i*128,128),128)
+    kp=k_ref[:,cs]; vT=v_ref[:,cs].T
+    bias=bias_ref[...]
+    khs=[]
+    for h in range(2):
+        khs.append(jnp.where((lane//64)==h,kp,jnp.where(lane==(64*(1-h)),bias,jnp.zeros_like(kp))))
+    for qi in range(L//bq):
+        qp=q_ref[pl.ds(qi*bq,bq),cs]*0.125
+        oT=[]
+        for h in range(2):
+            qh=jnp.where((lane//64)==h,qp,jnp.where(lane==(64*(1-h)),jnp.ones_like(qp),jnp.zeros_like(qp)))
+            sT=dot(khs[h],qh,1,1)
+            m=jnp.max(sT,axis=0,keepdims=True)
+            e=jnp.exp(sT-m)
+            l=jnp.sum(e,axis=0,keepdims=True)
+            p=(e*(1.0/l)).astype(BF)
+            oT.append(dot(vT[h*64:(h+1)*64],p,1,0))
+            lse_ref[i,h:h+1,qi*bq:(qi+1)*bq]=m+jnp.log(l)
+        o_ref[pl.ds(qi*bq,bq),cs]=jnp.concatenate(oT,axis=0).T.astype(BF)
+
+GCH=[(k*2*PIECE,2*PIECE,PIECE) for k in range(6)]+[(12*PIECE,PIECE,128)]
+
+def gather_steps(w_ref,g,zs,zr,fs,fr,ss,sr):
+    z,x,c,t=place(); zp,xp,yp,sp=peers(); n=len(GCH)
+    def cols(i): return pl.ds(GCH[i][0],GCH[i][1])
+    def ca(i): return pl.ds(GCH[i][0],GCH[i][2])
+    def cb(i): return pl.ds(GCH[i][0]+GCH[i][2],GCH[i][1]-GCH[i][2])
+    same=lambda r,s,q,d:rcopy(r,r,s,q,d)
+    Z=lambda i:[rcopy(w_ref.at[:,cols(i)],g.at[t,z,x,c,:,cols(i)],zs.at[i,d],zr.at[i,d],zp[d]) for d in range(3)]
+    A=lambda i:[same(g.at[t,:,x,c,:,ca(i)],fs.at[i,0],fr.at[i,0],xp),same(g.at[t,:,x,c,:,cb(i)],fs.at[i,1],fr.at[i,1],yp)]
+    B=lambda i:[same(g.at[t,:,:,c,:,ca(i)],fs.at[i,2],fr.at[i,2],yp),same(g.at[:,:,x,c,:,cb(i)],fs.at[i,3],fr.at[i,3],xp)]
+    S=lambda i:[same(g.at[:,:,:,c,:,cols(i)],ss.at[i],sr.at[i],sp)]
+    def begin():
+        for i in range(n):
+            g[t,z,x,c,:,cols(i)]=w_ref[:,cols(i)]
+        for i in range(n):
+            for q in Z(i): q.start()
+    def step(k):
+        if k<n:
+            for q in Z(k): q.wait_recv()
+            for q in A(k): q.start()
+        if 0<=k-1<n:
+            for q in A(k-1): q.wait_recv()
+            for q in B(k-1): q.start()
+        if 0<=k-2<n:
+            for q in B(k-2): q.wait_recv()
+            for q in S(k-2): q.start()
+        if 0<=k-3<n:
+            for q in S(k-3): q.wait_recv()
+    def finish():
+        for i in range(n):
+            for q in Z(i)+A(i)+B(i)+S(i): q.wait_send()
+    return begin,step,finish
+
+def front_kernel(w_ref,tok_hbm,cot_hbm,seg_ref,feat_ref,
+        q_o,k_o,v_o,o_o,lse_o,out_o,dmbT_o,abT_o,drbT_o,hid_o,dub_o,dr1_o,dob_o,hbT_o,wqkv_o,aux_o,sums_o,bup_o,time_o,
+        g,tok,cot,q,k,v,o,lse,own,bias,vecs,temb,hbT,gp,hid,dub,dmbT,abT,drbT,dr1,
+        zs,zr,fs,fr,ss,sr,lsem,osem,hsem):
+    z,x,c,t=place()
+    begin,step,finish=gather_steps(w_ref,g,zs,zr,fs,fr,ss,sr)
+    win=pl.ds(pl.multiple_of(t*512,512),L)
+    ltok=pltpu.make_async_copy(tok_hbm.at[win,:],tok,lsem.at[0]); ltok.start()
+    lcot=pltpu.make_async_copy(cot_hbm.at[win,:],cot,lsem.at[1]); lcot.start()
+    greet()
+    begin()
+    seg=seg_ref[:,pl.ds(pl.multiple_of(t*512,128),L)]
+    own_row=jnp.where(seg==t,1.0,0.0)
+    ownT=jnp.broadcast_to(own_row,(128,L)).T
+    own[...]=ownT
+    bias[...]=jnp.where(ownT>0.5,0.0,-1e30).astype(BF)
+    for s in range(4): step(s)
+    def vecblk(tt,n): return g[tt,n//4,(n//2)%2,n%2,32:48,256:384].astype(F32)
+    b0=[vecblk(0,n) for n in range(16)]; b1=[vecblk(1,n) for n in range(16)]
+    lv=spread(b0,48,6)
+    hv=jnp.concatenate([spread(b0,24,3),spread(b1,24,3)],axis=1)
+    vecs[0:16,:]=lv
+    vecs[16:32,:]=hv
+    bin_=spread(b0,32,4)[13:14,:]
+    inner=bin_
+    w1=jnp.concatenate([g[0,:,:,:,32:48,0:256].reshape(256,256),g[1,:,:,:,32:48,0:256].reshape(256,256)],axis=1)
+    inner=dot(feat_ref[...],w1,1,0)[0:1]+bin_
+    sig=1.0/(1.0+jnp.exp(-inner))
+    act=inner*sig
+    w2=jnp.concatenate([g[0,:,:,:,0:32,0:384].reshape(512,384),g[1,:,:,:,0:32,0:384].reshape(512,384)],axis=1)
+    actb=jnp.broadcast_to(act,(16,512)).astype(BF)
+    te=dot(actb,w2,1,0)[0:1]+lv[6:7]
+    temb[...]=jnp.broadcast_to(te,(8,D))
+    time_o[...]=jnp.concatenate([inner,sig,jnp.zeros((6,512),F32)],axis=0)
+    ltok.wait()
+    outs=[]
+    def emit(src,dst):
+        cp=pltpu.make_async_copy(src,dst,osem.at[len(outs)]); cp.start(); outs.append(cp)
+    def hid_rows(r,_):
+        rows=pl.ds(pl.multiple_of(r*RB,RB),RB)
+        hb=(tok[rows,:].astype(F32)+temb[0:1,:]).astype(BF)
+        hbT[:,rows]=hb.T
+        return 0
+    lax.fori_loop(0,L//RB,hid_rows,0)
+    def project(which,ref,brow):
+        def rows_body(r,_):
+            rows=pl.ds(pl.multiple_of(r*RB,RB),RB)
+            hb=(tok[rows,:].astype(F32)+temb[0:1,:]).astype(BF)
+            for tt in range(2):
+                val=dot(hb,g[tt,:,:,:,:,(1+which)*PIECE:(2+which)*PIECE].reshape(D,PIECE),1,0)
+                if brow is not None: val=val+vecs[brow:brow+1,tt*PIECE:(tt+1)*PIECE]
+                ref[rows,tt*PIECE:(tt+1)*PIECE]=val.astype(BF)
+            return 0
+        lax.fori_loop(0,L//RB,rows_body,0)
+    project(0,q,16+7)
+    emit(hbT,hbT_o); emit(q,q_o)
+    step(4)
+    project(1,k,None); project(2,v,16+8)
+    emit(k,k_o); emit(v,v_o)
+    emit(g.at[:,:,:,:,:,0:PIECE],aux_o); emit(g.at[:,:,:,:,:,PIECE:4*PIECE],wqkv_o)
+    def pair(i,_):
+        attend_pair(q,k,v,o,lse,bias,i)
+        for s in range(5):
+            @pl.when(i==s)
+            def _(): step(5+s)
+        return 0
+    lax.fori_loop(0,6,pair,0)
+    emit(o,o_o); emit(lse,lse_o)
+    lcot.wait()
+    for cp in outs: cp.wait()
+    done=len(outs)
+    out,dob=q,k
+    mid_body(g,tok,cot,o,own,vecs,temb,gp,hid,dub,out,dmbT,abT,drbT,dr1,dob,sums_o,bup_o,hid_o,dub_o,hsem)
+    for a,b in ((out,out_o),(dmbT,dmbT_o),(abT,abT_o),(drbT,drbT_o),(dr1,dr1_o),(dob,dob_o)): emit(a,b)
+    for cp in outs[done:]: cp.wait()
+    finish()
+
+def mid_body(g,tok,cot,o,own,vecs,temb,gp,hid,dub,out,dmbT,abT,drbT,dr1,dob,sums_o,bup_o,hid_o,dub_o,hsem):
+    def W(tt,piece,n=1): return g[tt,:,:,:,:,piece*PIECE:(piece+n)*PIECE].reshape(D,n*PIECE)
+    row=lambda r:vecs[r:r+1,:]
+    sums_o[...]=jnp.zeros((8,D),F32); bup_o[...]=jnp.zeros((8,4*D),F32)
+    csum=lambda a:jnp.sum(a,axis=0,keepdims=True)
+    def stage(buf,dst,r,which):
+        return pltpu.make_async_copy(buf.at[lax.rem(r,2)],dst.at[pl.ds(pl.multiple_of(r*RB,RB),RB),:],hsem.at[which,lax.rem(r,2)])
+    def block(r,_):
+        rows=pl.ds(pl.multiple_of(r*RB,RB),RB)
+        slot=lax.rem(r,2)
+        @pl.when(r>=2)
+        def _():
+            stage(hid,hid_o,r-2,0).wait(); stage(dub,dub_o,r-2,1).wait()
+        attn=dot(o[rows,0:PIECE],W(0,4),1,1)+dot(o[rows,PIECE:D],W(1,4),1,1)
+        r1=(tok[rows,:].astype(F32)+temb[0:1,:])+(attn+row(0))
+        x1,inv1=ln_stats(r1)
+        a=x1*row(1)+row(2)
+        ab=a.astype(BF)
+        abT[:,rows]=ab.T
+        mlp=row(3)
+        for tt in range(2):
+            for j in range(4):
+                cc=pl.ds((tt*4+j)*PIECE,PIECE)
+                u=dot(ab,W(tt,5+j),1,0)+vecs[16+9+j:16+10+j,tt*PIECE:(tt+1)*PIECE]
+                cdf=phi_cdf(u)
+                gp[:,cc]=cdf+u*jnp.exp(-0.5*u*u)*(1.0/math.sqrt(2*math.pi))
+                hid[slot,:,cc]=(u*cdf).astype(BF)
+            mlp=mlp+dot(hid[slot,:,tt*4*PIECE:(tt+1)*4*PIECE],W(tt,9,4),1,1)
+        stage(hid,hid_o,r,0).start()
+        x2,inv2=ln_stats(a+mlp)
+        out[rows,:]=(x2*row(4)+row(5)).astype(BF)
+        dy=jnp.where(own[rows,0:1]>0.5,cot[rows,:].astype(F32),0.0)
+        sums_o[4:5,:]+=csum(dy*x2); sums_o[5:6,:]+=csum(dy)
+        dr2=ln_back(row(4),dy,x2,inv2)
+        sums_o[3:4,:]+=csum(dr2)
+        dmb=dr2.astype(BF)
+        dmbT[:,rows]=dmb.T
+        da=dr2
+        for tt in range(2):
+            for j in range(4):
+                cc=pl.ds((tt*4+j)*PIECE,PIECE)
+                du=dot(dmb,W(tt,9+j),1,0)*gp[:,cc]
+                bup_o[0:1,cc]+=csum(du)
+                dub[slot,:,cc]=du.astype(BF)
+            da=da+dot(dub[slot,:,tt*4*PIECE:(tt+1)*4*PIECE],W(tt,5,4),1,1)
+        stage(dub,dub_o,r,1).start()
+        sums_o[1:2,:]+=csum(da*x1); sums_o[2:3,:]+=csum(da)
+        d1=ln_back(row(1),da,x1,inv1)
+        sums_o[0:1,:]+=csum(d1)
+        dr1[rows,:]=d1
+        drb=d1.astype(BF)
+        drbT[:,rows]=drb.T
+        for tt in range(2):
+            dob[rows,tt*PIECE:(tt+1)*PIECE]=dot(drb,W(tt,4),1,0).astype(BF)
+        return 0
+    lax.fori_loop(0,L//RB,block,0)
+    for r in (L//RB-2,L//RB-1):
+        stage(hid,hid_o,r,0).wait(); stage(dub,dub_o,r,1).wait()
+
+def front(w,tokens,cotangent,seg,featp,cid=0):
+    DMA=pltpu.SemaphoreType.DMA; n=len(GCH)
+    V=lambda s,d=BF:pltpu.VMEM(s,d)
+    A=pl.BlockSpec(memory_space=pl.ANY); M=pl.BlockSpec(memory_space=pltpu.VMEM)
+    big=lambda s,d=BF:jax.ShapeDtypeStruct(s,d)
+    row=(L,D); tr=(D,L)
+    G6=lambda w_:(NT,NZ,NX,NC,ROWS,w_)
+    return pl.pallas_call(front_kernel,
+        in_specs=[M,A,A,M,M],
+        out_specs=[A]*16+[M]*3,
+        out_shape=[big(row),big(row),big(row),big(row),big((6,2,L),F32),big(row),big(tr),big(tr),big(tr),big((L,4*D)),big((L,4*D)),
+            big(row,F32),big(row),big(tr),big(G6(3*PIECE)),big(G6(PIECE)),big((8,D),F32),big((8,4*D),F32),big((8,512),F32)],
+        scratch_shapes=[V(G6(WIDE)),V(row),V(row),V(row),V(row),V(row),V(row),V((6,2,L),F32),V((L,128),F32),V((L,128)),V((32,D),F32),V((8,D),F32),
+            V(tr),V((RB,4*D),F32),V((2,RB,4*D)),V((2,RB,4*D)),V(tr),V(tr),V(tr),V(row,F32),
+            DMA((n,3)),DMA((n,3)),DMA((n,4)),DMA((n,4)),DMA((n,)),DMA((n,)),DMA((2,)),DMA((20,)),DMA((2,2))],
+        compiler_params=pltpu.CompilerParams(collective_id=cid,has_side_effects=True,vmem_limit_bytes=63*2**20),name="front")(w,tokens,cotangent,seg,featp)
+
 def shards_fast(tokens,cotangent,segment_ids,timesteps,*params):
     masters=params[:9];moments=params[9:18];averages=params[18:]
     t=lax.axis_index("tensor")
-    g=gather(pack_weights(*masters),CHUNKS)
-    g=g.reshape(NT,16,ROWS,13*PIECE)
-    aux=g[...,:PIECE]
-    both=lambda a:jnp.concatenate([a[0],a[1]],axis=-1)
-    w2=both(aux[:,:,:32].reshape(NT,512,PIECE))
-    w1=both(aux[:,:,32:,:256].reshape(NT,256,256))
-    vec=aux[:,:,32:,256:].astype(F32)
-    lv=vec[0,:,0:7,0:48].transpose(1,0,2).reshape(7,D)
-    hv=vec[:,:,7:13,0:24].transpose(2,0,1,3).reshape(6,D)
-    b1=vec[0,:,13,0:32].reshape(1,512)
-    wide=g.reshape(NT,D,13*PIECE)
-    w_qkv=wide[...,PIECE:4*PIECE].reshape(NT,D,3,PIECE)
-    w_outT=wide[...,4*PIECE:5*PIECE]
-    w_up=wide[...,5*PIECE:9*PIECE]
-    w_downT=wide[...,9*PIECE:]
-
-    seg=lax.dynamic_slice_in_dim(segment_ids[0],t*512,L,0)
-    own=(seg==t)[:,None]
-    tok=lax.dynamic_slice_in_dim(tokens,t*512,L,0).astype(F32)
-    dy=jnp.where(own,lax.dynamic_slice_in_dim(cotangent,t*512,L,0).astype(F32),0.0)
     step=lax.dynamic_slice_in_dim(timesteps,t,1,1)[0]
     feat=time_features(step,TD).astype(BF)
-    featp=jnp.pad(feat.reshape(16,8),((0,0),(0,8))).reshape(1,256)
-    inner=dot(featp,w1,1,0)+b1
-    sig=jax.nn.sigmoid(inner)
-    act=(inner*sig).astype(BF)
-    temb=dot(act,w2,1,0)+lv[6:7]
-    h0=tok+temb
-    hb=h0.astype(BF)
-    proj=jnp.einsum("pd,tdce->pcte",hb,w_qkv,preferred_element_type=F32).reshape(L,3,D)
-    q=(proj[:,0]+hv[0]).astype(BF); k=proj[:,1].astype(BF); v=(proj[:,2]+hv[1]).astype(BF)
+    featp=jnp.broadcast_to(jnp.pad(feat.reshape(16,8),((0,0),(0,8))).reshape(1,256),(16,256))
+    q,k,v,o,lse,out_win,dmbT,abT,drbT,hid,dub,dr1,dob,hbT,wq6,aux6,sums,bups,tstate=front(pack_weights(*masters),tokens,cotangent,segment_ids,featp)
+    own=(lax.dynamic_slice_in_dim(segment_ids[0],t*512,L,0)==t)[:,None]
     bias=jnp.where(own,0.0,-1e30).astype(F32)
-    o,lse=call_fwd(fwdT,512,q,k,v,bias)
-    attn=jnp.einsum("pte,tfe->pf",o.reshape(L,NT,PIECE),w_outT,preferred_element_type=F32)+lv[0]
-    x1,inv1=ln_stats(h0+attn)
-    a=x1*lv[1]+lv[2]
-    ab=a.astype(BF)
-    bup=hv[2:].reshape(4,NT,PIECE).transpose(1,0,2).reshape(NT,4*PIECE)
-    u=jnp.einsum("pd,tdj->ptj",ab,w_up,preferred_element_type=F32)+bup
-    cdf=phi_cdf(u)
-    hid=(u*cdf).astype(BF)
-    mlp=jnp.einsum("ptj,tfj->pf",hid,w_downT,preferred_element_type=F32)+lv[3]
-    x2,inv2=ln_stats(a+mlp)
-    out_win=(x2*lv[4]+lv[5]).astype(BF)
-    g_gain2=jnp.sum(dy*x2,0); g_shift2=jnp.sum(dy,0)
-    dr2=ln_back(lv[4],dy,x2,inv2)
-    g_bdown=jnp.sum(dr2,0)
-    dmb=dr2.astype(BF)
-    g_down=jnp.einsum("pf,ptj->tfj",dmb,hid,preferred_element_type=F32)
-    dhid=jnp.einsum("pf,tfj->ptj",dmb,w_downT,preferred_element_type=F32)
-    du=dhid*(cdf+u*jnp.exp(-0.5*u*u)*(1.0/math.sqrt(2*math.pi)))
-    g_bup=jnp.sum(du,0)
-    dub=du.astype(BF)
-    g_up=jnp.einsum("pd,ptj->tdj",ab,dub,preferred_element_type=F32)
-    da=jnp.einsum("ptj,tdj->pd",dub,w_up,preferred_element_type=F32)+dr2
-    g_gain1=jnp.sum(da*x1,0); g_shift1=jnp.sum(da,0)
-    dr1=ln_back(lv[1],da,x1,inv1)
-    g_bo=jnp.sum(dr1,0)
-    drb=dr1.astype(BF)
-    g_out=jnp.einsum("pf,pte->tfe",drb,o.reshape(L,NT,PIECE),preferred_element_type=F32)
-    dob=jnp.einsum("pf,tfe->pte",drb,w_outT,preferred_element_type=F32).astype(BF).reshape(L,D)
+    w_qkv=wq6.reshape(NT,D,3,PIECE)
+    both=lambda a:jnp.concatenate([a[0],a[1]],axis=-1)
+    w2=both(aux6.reshape(NT,16,ROWS,PIECE)[:,:,:32].reshape(NT,512,PIECE))
+    inner=tstate[0:1];sig=tstate[1:2];act=(inner*sig).astype(BF)
+    featp=featp[:1]
+    g_bo,g_gain1,g_shift1,g_bdown,g_gain2,g_shift2=[sums[r] for r in range(6)]
+    g_bup=bups[0].reshape(NT,4*PIECE)
+    E=functools.partial(jnp.einsum,preferred_element_type=F32)
+    hidr=hid.reshape(L,NT,4*PIECE);dubr=dub.reshape(L,NT,4*PIECE)
+    g_down=E("fp,ptj->tfj",dmbT,hidr);g_up=E("dp,ptj->tdj",abT,dubr);g_out=E("fp,pte->tfe",drbT,o.reshape(L,NT,PIECE))
+    hb=hbT.T
     dq,dk,dv=call_bwd(bwdT,512,q,k,v,dob,bias,lse)
     g_bq=jnp.sum(dq,0); g_bv=jnp.sum(dv,0)
     dqkv=jnp.stack([dq,dk,dv],axis=1).astype(BF).reshape(L,3,NT,PIECE)

time: 658 us -> 479 us (0.73)
  matrix products: 99.8 us -> 34.1 us
  local copies, waits for them, and re-layouts: 127 us -> 71.6 us
  blocking collectives: 85.8 us -> 42.2 us
  other arithmetic: 78.6 us -> 55.9 us
  Pallas kernels: 243 us -> 256 us
    dot_general x10 -> x3, matrix products: 83.5 us -> 16.7 us  [the longest x1 8.38 us: shards_fast(): g_up = E('dp,ptj->tdj', abT, dubr)]
    psum x1, blocking collectives: 85.8 us -> 42.2 us  [shards_fast(): norm = jnp.sqrt(lax.psum(squares, ('dp', 'tensor')))]
    pallas_call x2 -> x1, Pallas kernels: 113 us -> 135 us  [front(): pl.pallas_call(front_kernel, in_specs=[M, A, A, M, M], out_specs=[A] * 16...]
    transpose x3 -> x0, local copies, waits for them, and re-layouts: 14.8 us -> none  [the longest x1 14.8 us: shards_fast(): jnp.einsum('pd,tdce->pcte', hb, w_qkv, preferred_element_type=F32)]
    reduce_sum x5 -> x0, other arithmetic: 11 us -> none  [the longest x1 4.78 us: shards_fast(): g_bdown = jnp.sum(dr2, 0)]
    unnamed x118 -> x94, local copies, waits for them, and re-layouts: 25.7 us -> 16.3 us
    pallas_call x1, Pallas kernels: 88.1 us -> 79.5 us  [scatter(): pl.pallas_call(functools.partial(scatter_kernel, chunks), in_specs=[pl.Bl...]
    slice x8 -> x2, local copies, waits for them, and re-layouts: 9.32 us -> 0.93 us  [the longest x1 0.93 us: shards_fast(): g_bup = bups[0].reshape(NT, 4 * PIECE)]
  transfers between devices with their start and end apart: 3 -> 3, of which waited for: 0 -> 0; matrix products, arithmetic and copies ran while one was open for 5% -> 31% of each run, Pallas kernels for 0% -> 26%
where the time goes in v2:
time: 479 us; the launch traced here: 472 us
  Pallas kernels  256 us (53%)
  local copies, waits for them, and re-layouts  71.6 us (15%)
  other arithmetic  55.9 us (12%)
  blocking collectives  42.2 us (9%)
  matrix products  34.1 us (7%)
  between operations  9.34 us (2%)
    pallas_call x1, Pallas kernels, front(): pl.pallas_call(front_kernel, in_specs=[M, A, A, M, M], out_specs=[A] * 16...  135 us
    pallas_call x1, Pallas kernels, scatter(): pl.pallas_call(functools.partial(scatter_kernel, chunks), in_specs=[pl.Bl...  79.5 us
    pallas_call x1, Pallas kernels, call_bwd(): pl.pallas_call(functools.partial(body, b), grid=(6,), in_specs=[pl.BlockS...  42.2 us
    psum x1, blocking collectives, shards_fast(): norm = jnp.sqrt(lax.psum(squares, ('dp', 'tensor')))  42.2 us
    unnamed x94, local copies, waits for them, and re-layouts  16.3 us
    concatenate x2, local copies, waits for them, and re-layouts, shards_fast(): jnp.concatenate([auxg, slab(g_qkv), slab(g_out), slab(g_up), slab(g_down)...  10.4 us
  transfers between devices with their start and end apart: 3, of which 0 were waited for; matrix products, arithmetic and copies ran while one was open for 31% of the time, Pallas kernels for 26%

profile of v2, /device:TPU:0, one launch (start us, length us, event | category | flops | bytes accessed | tf_op | source)
XLA Modules:
  0.0 471.9 jit_solution(17499569353350315264)
XLA Ops:
  10.5 134.7 %front.1 = (bf16[1024,768]{1,0:T(8,128)(2,1)}, bf16[1024,768]{1,0:T(8,128)(2,1)}, bf16[1024,768]{1,0:T(8,128)(2,1)}, bf16[1024,768]{1,0:T(8,128)(2,1)}, f32[6,2,...) custom-call(bf16[48,4992]{1,0:T(8,128)(2,1)} %copy-done.9, ...), custom_call_target="tpu_custom_call" | custom-call | tf_op jit(solution)/shard_map/front/pallas_call | solution.py:840
  147.7 42.2 %bwdT_512.1 = (f32[1024,768]{1,0:T(8,128)}, f32[1024,768]{1,0:T(8,128)}, f32[1024,768]{1,0:T(8,128)}) custom-call(bf16[1024,768]{1,0:T(8,128)(2,1)} %get-tuple-element.53.q_ref, bf16[1024,768]{1,0:T(8,128)(2,1)} %get-tuple-element.54.k_ref, bf16[1024,768]{1,0:T(8,128)(2,1)} %get-tuple-element.55.v_ref, bf16[1024,768]{1,0:T(8,128)(2,1)} %get-tuple-element.56.do_ref, ...), custom_call_target="tpu_custom_call" | custom-call | tf_op jit(solution)/shard_map/bwdT_512/pallas_call | solution.py:598
  189.9 3.2 fusion.68
  193.5 3.2 convert.62
  196.7 3.4 stack.21
  200.1 4.4 fusion.69
  204.5 4.4 stack.22
  210.2 8.5 %reshape.253 = bf16[2,768,3,384]{3,2,1,0:T(4,128)(2,1)} reshape(bf16[2,4,2,2,48,1152]{5,4,3,2,1,0:T(8,128)(2,1)} %get-tuple-element.61) | data formatting | bytes 7077888 | tf_op jit(solution)/shard_map/reshape | solution.py:859
  222.7 8.0 %fusion.70 = (bf16[768]{0:T(1024)(128)(2,1)S(1)}, bf16[1024,768]{1,0:T(8,128)(2,1)}) fusion(f32[1024,768]{1,0:T(8,128)} %get-tuple-element.62, bf16[1024,3,2,384]{3,0,2,1:T(8,128)(2,1)} %copy_dynamic-update-slice_fusion, bf16[2,768,3,384]{3,2,1,0:T(4,128)(2,1)S(1)} %copy-done.3), kind=kOutput, calls=%fused_computation.160 | convolution fusion | flops 3626237184 | bytes 12977664 | tf_op jit(solution)/shard_map/pcte,tdce->pd/dot_general | solution.py:874
  240.1 2.8 fusion.24
  244.5 6.7 %convert_bitcast_fusion = bf16[2,768,3,384]{1,3,0,2:T(8,128)(2,1)S(1)} fusion(bf16[1024,3,2,384]{3,0,2,1:T(8,128)(2,1)} %copy_dynamic-update-slice_fusion, bf16[768,1024]{1,0:T(8,128)(2,1)} %get-tuple-element.67), kind=kOutput, calls=%fused_computation.12 | convolution fusion | flops 3625648128 | bytes 9830400 | tf_op jit(solution)/shard_map/pd,pcte->tdce/dot_general | solution.py:873
  251.3 5.6 %copy.99 = bf16[2,768,3,384]{3,2,1,0:T(4,128)(2,1)} copy(bf16[2,768,3,384]{1,3,0,2:T(8,128)(2,1)S(1)} %convert_bitcast_fusion) | data formatting | bytes 7077888 | tf_op jit(solution)/shard_map/convert_element_type | solution.py:884
  256.9 7.9 %concatenate.87 = bf16[2,4,2,2,48,1152]{5,4,3,2,1,0:T(8,128)(2,1)S(1)} reshape(bf16[2,768,3,384]{3,2,1,0:T(4,128)(2,1)} %copy.99) | data formatting | bytes 7077888 | tf_op jit(solution)/shard_map/concatenate | solution.py:893
  264.8 2.6 fusion.74
  273.0 1.7 reshape.258
  274.7 1.7 multiply_convert_fusion
  276.4 2.7 reshape.255
  281.5 6.0 %maximum_maximum_fusion = bf16[2,16,48,384]{3,0,2,1:T(2,128)(2,1)S(1)} fusion(bf16[2,16,1,128]{3,0,2,1:T(2,128)(2,1)S(1)} %broadcast_in_dim.65, bf16[2,16,6,24]{3,0,2,1:T(2,128)(2,1)S(1)} %maximum_bitcast_fusion, bf16[2,16,7,128]{3,0,2,1:T(2,128)(2,1)S(1)} %broadcast_in_dim.63, bf16[2,16,16,256]{3,0,2,1:T(2,128)(2,1)} %bitcast.153, ...), kind=kLoop, calls=%fused_computation.33 | loop fusion | flops 11206656 | bytes 2339840 | tf_op jit(solution)/shard_map/concatenate | solution.py:891
  289.3 8.4 %fusion.6 = bf16[2,1536,768]{1,2,0:T(8,128)(2,1)S(1)} fusion(bf16[128,2,8,1536]{3,2,1,0:T(8,128)(2,1)} %bitcast.168, bf16[768,1024]{1,0:T(8,128)(2,1)S(1)} %copy-done.36), kind=kOutput, calls=%fused_computation.8 | convolution fusion | flops 4834197504 | bytes 12582912 | tf_op jit(solution)/shard_map/dp,ptj->tdj/dot_general | solution.py:868
  297.7 5.5 %fusion.9 = bf16[2,1536,768]{1,2,0:T(8,128)(2,1)S(1)} fusion(bf16[128,2,8,1536]{3,2,1,0:T(8,128)(2,1)S(1)} %bitcast.167, bf16[768,1024]{1,0:T(8,128)(2,1)S(1)} %copy-done.35), kind=kOutput, calls=%fused_computation.9 | convolution fusion | flops 4834197504 | bytes 12582912 | tf_op jit(solution)/shard_map/fp,ptj->tfj/dot_general | solution.py:868
  303.3 2.2 constant_dynamic-update-slice_fusion.6
  306.7 2.5 constant_dynamic-update-slice_fusion.4
  309.3 2.5 constant_dynamic-update-slice_fusion.3.g_hbm
  311.8 79.5 %scatter.1 = f32[48,4992]{1,0:T(8,128)} custom-call(bf16[2,4,2,2,48,4992]{5,4,3,2,1,0:T(8,128)(2,1)} %constant_dynamic-update-slice_fusion.3.g_hbm), custom_call_target="tpu_custom_call" | custom-call | tf_op jit(solution)/shard_map/scatter/pallas_call | solution.py:514
  392.7 1.6 multiply_reduce_fusion.2
  394.3 1.8 multiply_reduce_fusion
  408.1 42.2 %psum.7 = f32[]{:T(128)} all-reduce(f32[]{:T(128)S(6)} %add.163), channel_id=1, replica_groups=mesh['dp'=16,'tensor'=2] {'dp','tensor'}, use_global_device_ids=true, to_apply=%region_12.13 | all-reduce | flops 1 | bytes 8 | tf_op jit(solution)/shard_map/psum | solution.py:911
  459.2 1.8 add_multiply_fusion.2
  463.1 1.6 broadcast_select_fusion.3
  465.0 2.1 broadcast_select_fusion.1
  467.4 1.6 pad_maximum_fusion
  468.9 1.6 pad_maximum_fusion.1
  (182 shorter events, 57.8 us)
Async XLA Ops:
  0.7 9.0 %copy-start.11 = (f32[384,48]{0,1:T(8,128)S(1)}, f32[384,48]{0,1:T(8,128)}, u32[]{:S(2)}) copy-start(f32[384,48]{0,1:T(8,128)} %param.36) | copy-start | bytes 221188
  10.5 136.2 %copy-start.22 = (s32[1,1536]{1,0:T(1,128)S(1)}, s32[1,1536]{1,0:T(1,128)}, u32[]{:S(2)}) copy-start(s32[1,1536]{1,0:T(1,128)} %seg_ref.1) | copy-start | bytes 18436
  145.1 318.0 %collective-permute-start = (bf16[1024,768]{1,0:T(8,128)(2,1)}, bf16[1024,768]{1,0:T(8,128)(2,1)}, u32[]{:S(2)}, u32[]{:S(2)}) collective-permute-start(bf16[1024,768]{1,0:T(8,128)(2,1)} %get-tuple-element.52), channel_id=1, source_target_pairs={{0,1},{1,0},{2,3},{3,2},{4,5},{5,4},{6,7},{7,6},{8,9},{9,8},{10,11... | collective-permute-start | bytes 4718600 | tf_op jit(solution)/shard_map/ppermute | solution.py:895
  222.6 14.0 %copy-start.27 = (f32[8,768]{1,0:T(8,128)S(1)}, f32[8,768]{1,0:T(8,128)}, u32[]{:S(2)}) copy-start(f32[8,768]{1,0:T(8,128)} %get-tuple-element.65) | copy-start | bytes 73732
  222.6 15.4 %copy-start.10 = (bf16[2,4,2,2,48,384]{5,4,3,2,1,0:T(8,128)(2,1)S(1)}, bf16[2,4,2,2,48,384]{5,4,3,2,1,0:T(8,128)(2,1)}, u32[]{:S(2)}) copy-start(bf16[2,4,2,2,48,384]{5,4,3,2,1,0:T(8,128)(2,1)} %get-tuple-element.64) | copy-start | bytes 3538948
  230.7 8.5 %copy-start.4 = (bf16[1024,768]{1,0:T(8,128)(2,1)S(1)}, bf16[1024,768]{1,0:T(8,128)(2,1)}, u32[]{:S(2)}) copy-start(bf16[1024,768]{1,0:T(8,128)(2,1)} %get-tuple-element.68) | copy-start | bytes 4718596
  230.7 234.3 %collective-permute-start.1 = (bf16[1024,768]{1,0:T(8,128)(2,1)}, bf16[1024,768]{1,0:T(8,128)(2,1)}, u32[]{:S(2)}, u32[]{:S(2)}) collective-permute-start(bf16[1024,768]{1,0:T(8,128)(2,1)} %get-tuple-element.168), channel_id=1, source_target_pairs={{0,1},{1,0},{2,3},{3,2},{4,5},{5,4},{6,7},{7,6},{8,9},{9,8},{10,11... | collective-permute-start | bytes 4718600 | tf_op jit(solution)/shard_map/ppermute | solution.py:895
  287.7 10.0 %slice-start = ((s8[6291456]{0:T(1024)(128)(4,1)}), s8[4194304]{0:T(1024)(128)(4,1)S(1)}, s32[]{:S(2)}) async-start(s8[6291456]{0:T(1024)(128)(4,1)} %bitcast.165), calls=%async_computation | async-start | bytes 8388608
  289.3 8.4 %slice-start.1 = ((s8[6291456]{0:T(1024)(128)(4,1)}), s8[2097152]{0:T(1024)(128)(4,1)S(1)}, s32[]{:S(2)}) async-start(s8[6291456]{0:T(1024)(128)(4,1)} %bitcast.165), calls=%async_computation.1 | async-start | bytes 4194304
  289.3 8.4 %copy-start.35 = (bf16[768,1024]{1,0:T(8,128)(2,1)S(1)}, bf16[768,1024]{1,0:T(8,128)(2,1)}, u32[]{:S(2)}) copy-start(bf16[768,1024]{1,0:T(8,128)(2,1)} %get-tuple-element.73) | copy-start | bytes 4718596
  391.3 60.8 %copy-start.25 = (f32[7,48]{1,0:T(8,128)S(1)}, f32[7,48]{1,0:T(8,128)}, u32[]{:S(2)}) copy-start(f32[7,48]{1,0:T(8,128)} %param.43) | copy-start | bytes 4036
  391.3 60.8 %copy-start.28 = (f32[7,48]{1,0:T(8,128)S(1)}, f32[7,48]{1,0:T(8,128)}, u32[]{:S(2)}) copy-start(f32[7,48]{1,0:T(8,128)} %param.61) | copy-start | bytes 4036
  391.3 60.8 %copy-start.29 = (f32[7,48]{1,0:T(8,128)S(1)}, f32[7,48]{1,0:T(8,128)}, u32[]{:S(2)}) copy-start(f32[7,48]{1,0:T(8,128)} %param.52) | copy-start | bytes 4036
  391.3 61.4 %copy-start.21 = (f32[8,512]{1,0:T(8,128)S(1)}, f32[8,512]{1,0:T(8,128)}, u32[]{:S(2)}) copy-start(f32[8,512]{1,0:T(8,128)} %param.39) | copy-start | bytes 49156
  391.3 61.4 %copy-start.23 = (f32[8,512]{1,0:T(8,128)S(1)}, f32[8,512]{1,0:T(8,128)}, u32[]{:S(2)}) copy-start(f32[8,512]{1,0:T(8,128)} %param.57) | copy-start | bytes 49156
  391.3 61.4 %copy-start.24 = (f32[8,512]{1,0:T(8,128)S(1)}, f32[8,512]{1,0:T(8,128)}, u32[]{:S(2)}) copy-start(f32[8,512]{1,0:T(8,128)} %param.48) | copy-start | bytes 49156
  391.4 62.0 %copy-start = (f32[48,4992]{1,0:T(8,128)S(1)}, f32[48,4992]{1,0:T(8,128)}, u32[]{:S(2)}) copy-start(f32[48,4992]{1,0:T(8,128)} %scatter.1) | copy-start | bytes 2875396
  391.4 62.0 %copy-start.12 = (f32[384,48]{0,1:T(8,128)S(1)}, f32[384,48]{0,1:T(8,128)}, u32[]{:S(2)}) copy-start(f32[384,48]{0,1:T(8,128)} %param.36) | copy-start | bytes 221188
  391.4 62.0 %copy-start.19 = (f32[384,48]{0,1:T(8,128)S(1)}, f32[384,48]{0,1:T(8,128)}, u32[]{:S(2)}) copy-start(f32[384,48]{0,1:T(8,128)} %param.54) | copy-start | bytes 221188
  391.4 62.0 %copy-start.20 = (f32[384,48]{0,1:T(8,128)S(1)}, f32[384,48]{0,1:T(8,128)}, u32[]{:S(2)}) copy-start(f32[384,48]{0,1:T(8,128)} %param.45) | copy-start | bytes 221188
  391.4 62.7 %copy-start.8 = (f32[48,3,384]{2,0,1:T(8,128)S(1)}, f32[48,3,384]{2,0,1:T(8,128)}, u32[]{:S(2)}) copy-start(f32[48,3,384]{2,0,1:T(8,128)} %param.35) | copy-start | bytes 663556
  391.4 62.7 %copy-start.17 = (f32[48,3,384]{2,0,1:T(8,128)S(1)}, f32[48,3,384]{2,0,1:T(8,128)}, u32[]{:S(2)}) copy-start(f32[48,3,384]{2,0,1:T(8,128)} %param.53) | copy-start | bytes 663556
  391.4 62.7 %copy-start.18 = (f32[48,3,384]{2,0,1:T(8,128)S(1)}, f32[48,3,384]{2,0,1:T(8,128)}, u32[]{:S(2)}) copy-start(f32[48,3,384]{2,0,1:T(8,128)} %param.44) | copy-start | bytes 663556
  392.4 7.7 %collective-permute-start.2 = (bf16[48,384]{1,0:T(8,128)(2,1)S(1)}, bf16[48,384]{1,0:T(8,128)(2,1)S(1)}, u32[]{:S(2)}, u32[]{:S(2)}) collective-permute-start(bf16[48,384]{1,0:T(8,128)(2,1)S(1)} %slice.182), channel_id=1, source_target_pairs={{0,1},{1,0},{2,3},{3,2},{4,5},{5,4},{6,7},{7,6},{8,9},{9,8},{10,11... | collective-permute-start | bytes 110600 | tf_op jit(solution)/shard_map/ppermute | solution.py:895
  394.3 60.3 %copy-start.26 = (f32[6,1,24]{2,1,0:T(1,128)S(1)}, f32[6,1,24]{2,1,0:T(1,128)}, u32[]{:S(2)}) copy-start(f32[6,1,24]{2,1,0:T(1,128)} %param.42) | copy-start | bytes 1732
  394.3 60.3 %copy-start.30 = (f32[6,1,24]{2,1,0:T(1,128)S(1)}, f32[6,1,24]{2,1,0:T(1,128)}, u32[]{:S(2)}) copy-start(f32[6,1,24]{2,1,0:T(1,128)} %param.60) | copy-start | bytes 1732
  394.3 60.3 %copy-start.31 = (f32[6,1,24]{2,1,0:T(1,128)S(1)}, f32[6,1,24]{2,1,0:T(1,128)}, u32[]{:S(2)}) copy-start(f32[6,1,24]{2,1,0:T(1,128)} %param.51) | copy-start | bytes 1732
  404.8 49.9 %copy-start.32 = (f32[32]{0:T(128)S(1)}, f32[32]{0:T(128)}, u32[]{:S(2)}) copy-start(f32[32]{0:T(128)} %param.41) | copy-start | bytes 388
  404.8 49.9 %copy-start.33 = (f32[32]{0:T(128)S(1)}, f32[32]{0:T(128)}, u32[]{:S(2)}) copy-start(f32[32]{0:T(128)} %param.59) | copy-start | bytes 388
  404.8 49.9 %copy-start.34 = (f32[32]{0:T(128)S(1)}, f32[32]{0:T(128)}, u32[]{:S(2)}) copy-start(f32[32]{0:T(128)} %param.50) | copy-start | bytes 388
  454.5 6.5 %copy-start.6 = (f32[48,4,384]{2,1,0:T(4,128)S(1)}, f32[48,4,384]{2,1,0:T(4,128)}, u32[]{:S(2)}) copy-start(f32[48,4,384]{2,1,0:T(4,128)} %param.37) | copy-start | bytes 884740
  454.5 6.5 %copy-start.13 = (f32[48,4,384]{2,1,0:T(4,128)S(1)}, f32[48,4,384]{2,1,0:T(4,128)}, u32[]{:S(2)}) copy-start(f32[48,4,384]{2,1,0:T(4,128)} %param.55) | copy-start | bytes 884740
  (10 other events, 36.6 us)

commit v3 on v2

--- a/solution.py
+++ b/solution.py
@@ -847,6 +847,266 @@
             DMA((n,3)),DMA((n,3)),DMA((n,4)),DMA((n,4)),DMA((n,)),DMA((n,)),DMA((2,)),DMA((20,)),DMA((2,2))],
         compiler_params=pltpu.CompilerParams(collective_id=cid,has_side_effects=True,vmem_limit_bytes=63*2**20),name="front")(w,tokens,cotangent,seg,featp)
 
+RGR=[dict(g=0,r=0,w=768,a=384),dict(g=768,r=768,w=768,a=384),dict(g=1536,r=1536,w=768,a=384),dict(g=2304,r=2304,w=768,a=384),
+     dict(g=3072,r=3072,w=384,a=128),dict(g=0,r=3456,w=768,a=384),dict(g=768,r=4224,w=768,a=384)]
+_a=_b=0
+for _q in RGR:
+    _q["ao"]=_a; _q["bo"]=_b; _a+=_q["a"]; _b+=_q["w"]-_q["a"]
+RWA,RWB=_a,_b
+
+def scatter_steps(gb,rs,ra,rc,rb,rz,red,ss,sr,as_,ar,bs,br,zs,zr):
+    z,x,c,t=place(); zp,xp,yp,sp=peers()
+    def sl(i):
+        q=RGR[i]; g,r,w,a,ao,bo=q["g"],q["r"],q["w"],q["a"],q["ao"],q["bo"]
+        return dict(g=pl.ds(g,w),ga=pl.ds(g,a),gb=pl.ds(g+a,w-a),r=pl.ds(r,w),ra=pl.ds(r,a),rb=pl.ds(r+a,w-a),a=pl.ds(ao,a),b=pl.ds(bo,w-a))
+    def S(i):
+        k=sl(i); return [rcopy(gb.at[:,:,:,1-c,:,k["g"]],rs.at[:,:,:,:,k["r"]],ss.at[i],sr.at[i],sp)]
+    def A(i):
+        k=sl(i); return [rcopy(gb.at[:,:,1-x,c,:,k["ga"]],ra.at[:,:,:,k["a"]],as_.at[i,0],ar.at[i,0],xp),
+                         rcopy(gb.at[1-t,:,:,c,:,k["gb"]],rc.at[:,:,:,k["b"]],as_.at[i,1],ar.at[i,1],yp)]
+    def B(i):
+        k=sl(i); return [rcopy(gb.at[1-t,:,x,c,:,k["ga"]],rb.at[:,:,k["ra"]],bs.at[i,0],br.at[i,0],yp),
+                         rcopy(gb.at[t,:,1-x,c,:,k["gb"]],rb.at[:,:,k["rb"]],bs.at[i,1],br.at[i,1],xp)]
+    def Z(i):
+        k=sl(i); return [rcopy(gb.at[t,lax.rem(z+d+1,NZ),x,c,:,k["g"]],rz.at[d,:,k["r"]],zs.at[i,d],zr.at[i,d],zp[d]) for d in range(3)]
+    def go(cs):
+        for q in cs: q.start()
+    def got(cs):
+        for q in cs: q.wait_recv()
+    def sums(a,b): return (a.astype(F32)+b.astype(F32)).astype(BF)
+    def s_to_a(i):
+        got(S(i)); k=sl(i)
+        def body(n,_):
+            tt=lax.div(n,8); zz=lax.rem(lax.div(n,2),4); xx=lax.rem(n,2)
+            gb[tt,zz,xx,c,:,k["g"]]=sums(gb[tt,zz,xx,c,:,k["g"]],rs[tt,zz,xx,:,k["r"]])
+            return 0
+        lax.fori_loop(0,16,body,0)
+        go(A(i))
+    def a_to_b(i):
+        got(A(i)); k=sl(i)
+        def body(n,_):
+            a=lax.div(n,4); b=lax.rem(n,4)
+            gb[a,b,x,c,:,k["ga"]]=sums(gb[a,b,x,c,:,k["ga"]],ra[a,b,:,k["a"]])
+            zz=lax.div(n,2); xx=lax.rem(n,2)
+            gb[t,zz,xx,c,:,k["gb"]]=sums(gb[t,zz,xx,c,:,k["gb"]],rc[zz,xx,:,k["b"]])
+            return 0
+        lax.fori_loop(0,8,body,0)
+        go(B(i))
+    def b_to_z(i):
+        got(B(i)); k=sl(i)
+        def body(n,_):
+            gb[t,n,x,c,:,k["g"]]=sums(gb[t,n,x,c,:,k["g"]],rb[n,:,k["r"]])
+            return 0
+        lax.fori_loop(0,4,body,0)
+        go(Z(i))
+    def z_end(i):
+        got(Z(i)); k=sl(i)
+        acc=gb[t,z,x,c,:,k["g"]].astype(F32)
+        for d in range(3): acc=acc+rz[d,:,k["r"]].astype(F32)
+        red[:,k["r"]]=acc
+    def drain(i):
+        for q in S(i)+A(i)+B(i)+Z(i): q.wait_send()
+    return S,go,s_to_a,a_to_b,b_to_z,z_end,drain
+
+def attend_back(q_ref,k_ref,v_ref,do_ref,lse_ref,bias_ref,hvs,i,bq=512):
+    lane=lax.broadcasted_iota(jnp.int32,(1,128),1)
+    cs=pl.ds(pl.multiple_of(i*128,128),128)
+    kp=k_ref[:,cs]; vp=v_ref[:,cs]; bias=bias_ref[...]
+    khs=[];vhs=[]
+    for h in range(2):
+        sel=(lane//64)==h; one=lane==(64*(1-h))
+        khs.append(jnp.where(sel,kp,jnp.where(one,bias,jnp.zeros_like(kp))))
+        vhs.append(jnp.where(sel,vp,jnp.zeros_like(vp)))
+    kT=kp.T
+    dk=[None,None];dv=[None,None]; sq=None
+    for qi in range(L//bq):
+        rows=pl.ds(qi*bq,bq)
+        qp=q_ref[rows,cs]*0.125; dop=do_ref[rows,cs]
+        dqT=[]
+        for h in range(2):
+            sel=(lane//64)==h; one=lane==(64*(1-h))
+            zero=jnp.zeros_like(qp)
+            qh=jnp.where(sel,qp,jnp.where(one,jnp.ones_like(qp),zero))
+            doh=jnp.where(sel,dop,zero)
+            qz=jnp.where(sel,qp,zero)
+            sT=dot(khs[h],qh,1,1)
+            p=jnp.exp(sT-lse_ref[i,h:h+1,qi*bq:(qi+1)*bq])
+            dp=dot(vhs[h],doh,1,1)
+            d=jnp.sum(p*dp,axis=0,keepdims=True)
+            ds=(p*(dp-d)).astype(BF)
+            pb=p.astype(BF)
+            a=dot(pb,doh,1,0); dv[h]=a if dv[h] is None else dv[h]+a
+            a=dot(ds,qz,1,0); dk[h]=a if dk[h] is None else dk[h]+a
+            dqT.append(dot(kT[h*64:(h+1)*64],ds,1,0))
+        dq=jnp.concatenate(dqT,axis=0).T*0.125
+        s=jnp.sum(dq,axis=0,keepdims=True); sq=s if sq is None else sq+s
+        q_ref[rows,cs]=dq.astype(BF)
+    k_ref[:,cs]=(dk[0]+dk[1]).astype(BF)
+    dvv=dv[0]+dv[1]
+    v_ref[:,cs]=dvv.astype(BF)
+    hvs[0:1,cs]=sq
+    hvs[1:2,cs]=jnp.sum(dvv,axis=0,keepdims=True)
+
+def unspread(src,w,n):
+    lane=lax.broadcasted_iota(jnp.int32,(16,128),1)
+    tile,s=divmod(n*w,128)
+    wide=src[:,tile*128:(tile+2)*128]
+    if s: wide=pltpu.roll(wide,256-s,1)
+    return jnp.where(lane<w,wide[:,:128],0.0)
+
+def back_kernel(q_h,k_h,v_h,do_h,o_h,lse_h,dmbT_h,abT_h,drbT_h,hbT_h,hid_h,dub_h,dr1_h,wqkv_h,aux_h,out_h,seg_ref,feat_ref,sums_ref,bup_ref,time_ref,
+        in_o,inp_o,outp_o,red,auxp,tot,
+        q,k,v,do,lse,bias,st,ta,tb,wq,dr1,aux,inw,hvs,lvs,hsrc,bsrc,auxm,nv,nr,nz,
+        gb,rs,ra,rc,rb,rz,ss,sr,as_,ar,bs,br,zs,zr,ls,ts,xs,ns,nrs):
+    z,x,c,t=place(); zp,xp,yp,sp=peers()
+    S,go,s_to_a,a_to_b,b_to_z,z_end,drain=scatter_steps(gb,rs,ra,rc,rb,rz,red,ss,sr,as_,ar,bs,br,zs,zr)
+    def load(src,dst,n):
+        return pltpu.make_async_copy(src,dst,ls.at[n])
+    LQ=[load(q_h,q,0),load(k_h,k,1),load(v_h,v,2),load(do_h,do,3),load(lse_h,lse,4)]
+    LW=[load(wqkv_h,wq,5),load(dr1_h,dr1,6),load(aux_h,aux,7)]
+    def tcopy(src,buf,n): return pltpu.make_async_copy(src,buf,ts.at[n])
+    def stage(src,cols,n):
+        return [pltpu.make_async_copy(src.at[:,pl.ds(cs,PIECE)],st.at[s],ts.at[n+s]) for s,cs in enumerate(cols)]
+    pc=lambda j:[tt*4*PIECE+jj*PIECE for jj in (j,j+1) for tt in range(2)]
+    ST=[stage(hid_h,pc(0),4),stage(hid_h,pc(2),8),stage(dub_h,pc(0),4),stage(dub_h,pc(2),8),stage(o_h,[0,PIECE],4)]
+    for q_ in [tcopy(dmbT_h,ta,0),*ST[0],tcopy(abT_h,tb,1)]+LQ+LW: q_.start()
+    greet()
+    cout=rcopy(out_h,outp_o,xs.at[0],xs.at[1],yp); cout.start()
+    seg=seg_ref[:,pl.ds(pl.multiple_of(t*512,128),L)]
+    bias[...]=jnp.broadcast_to(jnp.where(seg==t,0.0,-1e30),(128,L)).T.astype(BF)
+    def compute(i,lhs,n):
+        base=RGR[i]["g"]
+        for q_ in ST[i]: q_.wait()
+        def body(s,_):
+            tt=lax.rem(s,2); cs=pl.ds(pl.multiple_of(base+lax.div(s,2)*PIECE,128),PIECE)
+            gb[tt,:,:,:,:,cs]=dot(lhs[...],st[s],1,0).astype(BF).reshape(NZ,NX,NC,ROWS,PIECE)
+            return 0
+        lax.fori_loop(0,n,body,0)
+        if i+1<len(ST):
+            for q_ in ST[i+1]: q_.start()
+        go(S(i))
+    tcopy(dmbT_h,ta,0).wait()
+    compute(0,ta,4)
+    compute(1,ta,4)
+    tcopy(drbT_h,ta,2).start()
+    tcopy(abT_h,tb,1).wait()
+    for q_ in LQ: q_.wait()
+    def pair(i,_):
+        @pl.when(i==0)
+        def _():
+            s_to_a(0); s_to_a(1); compute(2,tb,4)
+        @pl.when(i==1)
+        def _():
+            a_to_b(0); a_to_b(1); s_to_a(2); compute(3,tb,4); tcopy(hbT_h,tb,3).start()
+        @pl.when(i==2)
+        def _():
+            b_to_z(0); b_to_z(1); a_to_b(2); s_to_a(3); tcopy(drbT_h,ta,2).wait(); compute(4,ta,2)
+        @pl.when(i==3)
+        def _():
+            z_end(0); z_end(1); b_to_z(2); a_to_b(3); s_to_a(4)
+        @pl.when(i==4)
+        def _():
+            z_end(2); b_to_z(3); a_to_b(4)
+        @pl.when(i==5)
+        def _():
+            z_end(3); b_to_z(4)
+        attend_back(q,k,v,do,lse,bias,hvs,i)
+        return 0
+    lax.fori_loop(0,6,pair,0)
+    z_end(4)
+    for i in range(5): drain(i)
+    tcopy(hbT_h,tb,3).wait()
+    def qkv_grad(i,pairs):
+        for n,ref in enumerate(pairs):
+            for tt in range(2):
+                cs=RGR[i]["g"]+n*PIECE
+                gb[tt,:,:,:,:,cs:cs+PIECE]=dot(tb[...],ref[:,tt*PIECE:(tt+1)*PIECE],1,0).astype(BF).reshape(NZ,NX,NC,ROWS,PIECE)
+    qkv_grad(5,[q,k]); go(S(5))
+    for q_ in LW: q_.wait()
+    lvs[...]=jnp.zeros((16,D+128),F32)
+    lvs[0:6,0:D]=sums_ref[0:6,:]
+    def rows_body(r,_):
+        rows=pl.ds(pl.multiple_of(r*RB,RB),RB)
+        acc=dr1[rows,:]
+        for n,ref in enumerate((q,k,v)):
+            for tt in range(2):
+                acc=acc+dot(ref[rows,tt*PIECE:(tt+1)*PIECE],wq[tt,:,:,:,:,n*PIECE:(n+1)*PIECE].reshape(D,PIECE),1,1)
+        inw[rows,:]=acc.astype(BF)
+        lvs[6:7,0:D]+=jnp.sum(acc,axis=0,keepdims=True)
+        return 0
+    lax.fori_loop(0,L//RB,rows_body,0)
+    cin=rcopy(inw,inp_o,xs.at[2],xs.at[3],yp); cin.start()
+    cinl=pltpu.make_async_copy(inw,in_o,ls.at[8]); cinl.start()
+    s_to_a(5)
+    qkv_grad(6,[v])
+    dtb=lvs[6:7,0:D].astype(BF)
+    inner=time_ref[0:1,:]; sig=time_ref[1:2,:]
+    w2=jnp.concatenate([aux[0,:,:,:,0:32,:].reshape(512,PIECE),aux[1,:,:,:,0:32,:].reshape(512,PIECE)],axis=1)
+    dinner=dot(jnp.broadcast_to(dtb,(16,D)),w2,1,1)[0:1]*(sig*(1.0+inner*(1.0-sig)))
+    act=(inner*sig).astype(BF).astype(F32)
+    actc=jnp.broadcast_to(act,(128,512)).T[:,0:1]
+    featc=jnp.broadcast_to(feat_ref[0:1,:].astype(F32),(128,256)).T[:,0:1]
+    dinb=dinner.astype(BF).astype(F32); dtf=dtb.astype(F32)
+    hsrc[...]=jnp.zeros((16,2*(PIECE+128)),F32)
+    for tt in range(2):
+        o0=tt*(PIECE+128); cc=slice(tt*PIECE,(tt+1)*PIECE)
+        hsrc[7:9,o0:o0+PIECE]=hvs[0:2,cc]
+        for j in range(4): hsrc[9+j:10+j,o0:o0+PIECE]=bup_ref[0:1,(tt*4+j)*PIECE:(tt*4+j+1)*PIECE]
+    bsrc[...]=jnp.zeros((16,640),F32)
+    bsrc[13:14,0:512]=dinner
+    base=RGR[6]["g"]+PIECE
+    for tt in range(2):
+        gb[tt,:,:,:,0:32,base:base+PIECE]=(actc*dtf[:,tt*PIECE:(tt+1)*PIECE]).astype(BF).reshape(NZ,NX,NC,32,PIECE)
+        gb[tt,:,:,:,32:48,base:base+256]=(featc*dinb[:,tt*256:(tt+1)*256]).astype(BF).reshape(NZ,NX,NC,16,256)
+        hs=hsrc[:,tt*(PIECE+128):(tt+1)*(PIECE+128)]
+        for n in range(16):
+            blk=unspread(lvs[...],48,n)+unspread(hs,24,n)+unspread(bsrc[...],32,n)
+            gb[tt,n//4,(n//2)%2,n%2,32:48,base+256:base+PIECE]=blk.astype(BF)
+    go(S(6))
+    a_to_b(5)
+    s_to_a(6)
+    b_to_z(5)
+    a_to_b(6)
+    z_end(5)
+    b_to_z(6)
+    z_end(6)
+    am=red[:,12*PIECE:13*PIECE].astype(BF)
+    auxm[...]=am
+    cax=rcopy(auxm,auxp,xs.at[4],xs.at[5],yp); cax.start()
+    af=am.astype(F32)
+    ri=lax.broadcasted_iota(jnp.int32,(ROWS,PIECE),0); ci=lax.broadcasted_iota(jnp.int32,(ROWS,PIECE),1)
+    dup=(ri>=32)&(ci>=256)&((ri<39)|(ri==45))
+    sqa=jnp.where(dup&(t!=0),0.0,af*af)
+    big=red[:,0:12*PIECE]
+    part=jnp.sum(sqa)+jnp.sum(big*big)
+    nv[0]=jnp.full((8,128),part,F32)
+    for s,peer in enumerate((yp,xp,sp)):
+        cp=rcopy(nv.at[s],nr.at[s],ns.at[s],nrs.at[s],peer); cp.start(); cp.wait()
+        nv[s+1]=nv[s]+nr[s]
+    cz=[rcopy(nv.at[3],nz.at[z],ns.at[3+d],nrs.at[3+d],zp[d]) for d in range(3)]
+    for q_ in cz: q_.start()
+    nz[z]=nv[3]
+    for q_ in cz: q_.wait()
+    tot[...]=((nz[0]+nz[1])+nz[2])+nz[3]
+    cax.wait(); cin.wait(); cinl.wait(); cout.wait()
+    for i in (5,6): drain(i)
+
+def back(q,k,v,dob,o,lse,dmbT,abT,drbT,hbT,hid,dub,dr1,wqkv,aux,out_win,seg,featp,sums,bups,tstate,cid=1):
+    DMA=pltpu.SemaphoreType.DMA; n=len(RGR)
+    V=lambda s,d=BF:pltpu.VMEM(s,d)
+    A=pl.BlockSpec(memory_space=pl.ANY); M=pl.BlockSpec(memory_space=pltpu.VMEM)
+    sd=jax.ShapeDtypeStruct; row=(L,D); tr=(D,L)
+    return pl.pallas_call(back_kernel,
+        in_specs=[A]*16+[M]*5,out_specs=[A]*3+[M]*3,
+        out_shape=[sd(row,BF),sd(row,BF),sd(row,BF),sd((ROWS,WIDE),F32),sd((ROWS,PIECE),BF),sd((8,128),F32)],
+        scratch_shapes=[V(row),V(row),V(row),V(row),V((6,2,L),F32),V((L,128)),V((4,L,PIECE)),V(tr),V(tr),V((NT,NZ,NX,NC,ROWS,3*PIECE)),V(row,F32),
+            V((NT,NZ,NX,NC,ROWS,PIECE)),V(row),V((8,D),F32),V((16,D+128),F32),V((16,2*(PIECE+128)),F32),V((16,640),F32),V((ROWS,PIECE)),
+            V((4,8,128),F32),V((3,8,128),F32),V((4,8,128),F32),
+            V((NT,NZ,NX,NC,ROWS,9*PIECE)),V((NT,NZ,NX,ROWS,WIDE)),V((NT,NZ,ROWS,RWA)),V((NZ,NX,ROWS,RWB)),V((NZ,ROWS,WIDE)),V((3,ROWS,WIDE)),
+            DMA((n,)),DMA((n,)),DMA((n,2)),DMA((n,2)),DMA((n,2)),DMA((n,2)),DMA((n,3)),DMA((n,3)),DMA((9,)),DMA((12,)),DMA((6,)),DMA((6,)),DMA((6,))],
+        compiler_params=pltpu.CompilerParams(collective_id=cid,has_side_effects=True,vmem_limit_bytes=63*2**20),name="back")(
+            q,k,v,dob,o,lse,dmbT,abT,drbT,hbT,hid,dub,dr1,wqkv,aux,out_win,seg,featp,sums,bups,tstate)
+
 def shards_fast(tokens,cotangent,segment_ids,timesteps,*params):
     masters=params[:9];moments=params[9:18];averages=params[18:]
     t=lax.axis_index("tensor")
@@ -854,71 +1114,29 @@
     feat=time_features(step,TD).astype(BF)
     featp=jnp.broadcast_to(jnp.pad(feat.reshape(16,8),((0,0),(0,8))).reshape(1,256),(16,256))
     q,k,v,o,lse,out_win,dmbT,abT,drbT,hid,dub,dr1,dob,hbT,wq6,aux6,sums,bups,tstate=front(pack_weights(*masters),tokens,cotangent,segment_ids,featp)
-    own=(lax.dynamic_slice_in_dim(segment_ids[0],t*512,L,0)==t)[:,None]
-    bias=jnp.where(own,0.0,-1e30).astype(F32)
-    w_qkv=wq6.reshape(NT,D,3,PIECE)
-    both=lambda a:jnp.concatenate([a[0],a[1]],axis=-1)
-    w2=both(aux6.reshape(NT,16,ROWS,PIECE)[:,:,:32].reshape(NT,512,PIECE))
-    inner=tstate[0:1];sig=tstate[1:2];act=(inner*sig).astype(BF)
-    featp=featp[:1]
-    g_bo,g_gain1,g_shift1,g_bdown,g_gain2,g_shift2=[sums[r] for r in range(6)]
-    g_bup=bups[0].reshape(NT,4*PIECE)
-    E=functools.partial(jnp.einsum,preferred_element_type=F32)
-    hidr=hid.reshape(L,NT,4*PIECE);dubr=dub.reshape(L,NT,4*PIECE)
-    g_down=E("fp,ptj->tfj",dmbT,hidr);g_up=E("dp,ptj->tdj",abT,dubr);g_out=E("fp,pte->tfe",drbT,o.reshape(L,NT,PIECE))
-    hb=hbT.T
-    dq,dk,dv=call_bwd(bwdT,512,q,k,v,dob,bias,lse)
-    g_bq=jnp.sum(dq,0); g_bv=jnp.sum(dv,0)
-    dqkv=jnp.stack([dq,dk,dv],axis=1).astype(BF).reshape(L,3,NT,PIECE)
-    g_qkv=jnp.einsum("pd,pcte->tdce",hb,dqkv,preferred_element_type=F32)
-    dh0=jnp.einsum("pcte,tdce->pd",dqkv,w_qkv,preferred_element_type=F32)+dr1
-    in_win=dh0.astype(BF)
-    dtemb=jnp.sum(dh0,0,keepdims=True)
-    dtb=dtemb.astype(BF)
-    g_w2=dot(act,dtb,0,0)
-    dinner=dot(dtb,w2,1,1)*(sig*(1.0+inner*(1.0-sig)))
-    g_w1=dot(featp,dinner.astype(BF),0,0)
-    g_lv=jnp.stack([g_bo,g_gain1,g_shift1,g_bdown,g_gain2,g_shift2,dtemb[0]],0)
-    g_bup=g_bup.reshape(NT,4,PIECE).transpose(1,0,2).reshape(4,D)
-    g_hv=jnp.concatenate([g_bq[None],g_bv[None],g_bup],0)
-    low=lambda a:a.astype(BF)
-    padl=lambda a:jnp.pad(low(a),((0,0),)*3+((0,128-a.shape[-1]),))
-    lvp=jnp.broadcast_to(padl(g_lv.reshape(7,16,48).transpose(1,0,2)[None]),(NT,16,7,128))
-    hvp=padl(g_hv.reshape(6,NT,16,24).transpose(1,2,0,3))
-    b1p=jnp.broadcast_to(padl(dinner.reshape(1,16,1,32)),(NT,16,1,128))
-    vecp=jnp.concatenate([lvp,hvp,b1p,jnp.zeros((NT,16,2,128),BF)],axis=2)
-    split=lambda a,r,w:low(a).reshape(16,r,NT,w).transpose(2,0,1,3)
-    auxg=jnp.concatenate([split(g_w2,32,PIECE),jnp.concatenate([split(g_w1,16,256),vecp],axis=3)],axis=2)
-    slab=lambda a:low(a).reshape(NT,16,ROWS,-1)
-    big=jnp.concatenate([auxg,slab(g_qkv),slab(g_out),slab(g_up),slab(g_down)],axis=3).reshape(NT,NZ,NX,NC,ROWS,13*PIECE)
-    red=scatter(big,CHUNKS)
-    swap=lambda a:lax.ppermute(a,"tensor",[(0,1),(1,0)])
-    aux_mine=red[:,:PIECE].astype(BF)
-    aux_peer=swap(aux_mine)
+    in_win,in_peer,out_peer,red,aux_peer,total=back(q,k,v,dob,o,lse,dmbT,abT,drbT,hbT,hid,dub,dr1,wq6,aux6,out_win,segment_ids,featp,sums,bups,tstate)
+    aux_mine=red[:,12*PIECE:].astype(BF)
     aux0=jnp.where(t==0,aux_mine,aux_peer).astype(F32); aux1=jnp.where(t==0,aux_peer,aux_mine).astype(F32)
-    r_qkv=red[:,PIECE:4*PIECE].reshape(ROWS,3,PIECE)
-    r_out=red[:,4*PIECE:5*PIECE].T
-    r_up=red[:,5*PIECE:9*PIECE].reshape(ROWS,4,PIECE)
-    r_down=red[:,9*PIECE:].reshape(ROWS,4,PIECE).transpose(1,2,0)
+    r_down=red[:,0:4*PIECE].reshape(ROWS,4,PIECE).transpose(1,2,0)
+    r_up=red[:,4*PIECE:8*PIECE].reshape(ROWS,4,PIECE)
+    r_out=red[:,8*PIECE:9*PIECE].T
+    r_qkv=red[:,9*PIECE:12*PIECE].reshape(ROWS,3,PIECE)
     r_w2=jnp.concatenate([aux0[:32],aux1[:32]],axis=1)
     r_w1=jnp.concatenate([aux0[32:40,:256],aux1[32:40,:256]],axis=1)
     r_lv=aux0[32:39,256:304]
     r_b1=aux0[45,256:288]
     r_hv=jnp.where(t==0,aux0,aux1)[39:45,256:280].reshape(6,1,24)
     grads=(r_qkv,r_out,r_up,r_down,r_w1,r_w2,r_b1,r_hv,r_lv)
-    sq=lambda a:jnp.sum(a*a)
-    squares=sum(sq(grads[i]) for i in (0,1,2,3,7))+0.5*sum(sq(grads[i]) for i in (4,5,6,8))
-    norm=jnp.sqrt(lax.psum(squares,("dp","tensor")))
+    norm=jnp.sqrt(total[0,0])
     factor=1.0/jnp.maximum(norm,1.0)
     rate=4.0*math.sqrt(MPARAMS/D)
     new=[advance(m,v_,a_,g_,factor,rate) for m,v_,a_,g_ in zip(masters,moments,averages,grads)]
 
-    def whole(win):
-        peer=swap(win)
+    def whole(win,peer):
         lo=jnp.where(t==0,win,peer); hi=jnp.where(t==0,peer,win)
         mid=jnp.where((segment_ids[0,512:1024]==0)[:,None],lo[512:],hi[:512])
         return jnp.concatenate([lo[:512],mid,hi[512:]],axis=0)
-    return (whole(out_win),whole(in_win),norm)+tuple(n[0] for n in new)+tuple(n[1] for n in new)+tuple(n[2] for n in new)
+    return (whole(out_win,out_peer),whole(in_win,in_peer),norm)+tuple(n[0] for n in new)+tuple(n[1] for n in new)+tuple(n[2] for n in new)
 
 
 def solution(mesh):

time: 479 us -> 349 us (0.73); the launches traced: 472 us -> 349 us
  Pallas kernels: 256 us -> 319 us
  local copies, waits for them, and re-layouts: 71.6 us -> 8.98 us
  blocking collectives: 42.2 us -> 0 us
  other arithmetic: 55.9 us -> 18.2 us
  matrix products: 34.1 us -> 0 us
  between operations: 9.34 us -> 3.11 us
    pallas_call x2 -> x1, Pallas kernels: 122 us -> 184 us  [back(): pl.pallas_call(back_kernel, in_specs=[A] * 16 + [M] * 5, out_specs=[A] *...]
    psum x1 -> x0, blocking collectives: 42.2 us -> none  [shards_fast(): norm = jnp.sqrt(lax.psum(squares, ('dp', 'tensor')))]
    dot_general x6 -> x0, matrix products: 34.1 us -> none  [the longest x1 8.38 us: shards_fast(): g_up = E('dp,ptj->tdj', abT, dubr)]
    reduce_sum x10 -> x0, other arithmetic: 15.5 us -> none  [the longest x8 7.9 us: shards_fast(): sq = lambda a: jnp.sum(a * a)]
    reshape x4 -> x0, local copies, waits for them, and re-layouts: 13.9 us -> none  [the longest x1 8.52 us: shards_fast(): w_qkv = wq6.reshape(NT, D, 3, PIECE)]
    concatenate x10 -> x0, local copies, waits for them, and re-layouts: 12.1 us -> none  [the longest x2 10.4 us: shards_fast(): jnp.concatenate([auxg, slab(g_qkv), slab(g_out), slab(g_up), slab(g_down)...]
    another operation x8 -> x0, local copies, waits for them, and re-layouts: 11 us -> none  [the longest x4 9.55 us: shards_fast(): dqkv = jnp.stack([dq, dk, dv], axis=1).astype(BF).reshape(L, 3, NT, PIECE)]
    unnamed x94 -> x78, local copies, waits for them, and re-layouts: 16.3 us -> 5.93 us
  transfers between devices with their start and end apart: 3 -> 0, of which waited for: 0 -> 0; matrix products, arithmetic and copies ran while one was open for 31% -> 0% of each run, Pallas kernels for 26% -> 0%
where the time goes in v3:
time: 349 us
  Pallas kernels  319 us (91%)
  other arithmetic  18.2 us (5%)
  local copies, waits for them, and re-layouts  8.98 us (3%)
    pallas_call x1, Pallas kernels, back(): pl.pallas_call(back_kernel, in_specs=[A] * 16 + [M] * 5, out_specs=[A] *...  184 us
    pallas_call x1, Pallas kernels, front(): pl.pallas_call(front_kernel, in_specs=[M, A, A, M, M], out_specs=[A] * 16...  134 us

profile of v3, /device:TPU:0, one launch (start us, length us, event | category | flops | bytes accessed | tf_op | source)
XLA Modules:
  0.0 349.0 jit_solution(6207795563621401870)
XLA Ops:
  0.7 0.8 convert_element_type.62
  1.5 0.7 copy.120
  2.2 0.7 convert_element_type.63
  2.8 0.7 convert_bitcast_fusion.2
  3.5 0.8 dynamic-slice_convert_fusion
  4.3 1.0 convert_bitcast_fusion.1
  5.3 0.9 bitcast_dynamic-update-slice_fusion
  6.2 1.0 convert_element_type.70
  7.4 0.6 fusion.35
  8.1 0.7 sine_convert_fusion
  9.0 0.6 broadcast_in_dim.28.feat_ref
  9.7 134.5 %front.1 = (bf16[1024,768]{1,0:T(8,128)(2,1)}, bf16[1024,768]{1,0:T(8,128)(2,1)}, bf16[1024,768]{1,0:T(8,128)(2,1)}, bf16[1024,768]{1,0:T(8,128)(2,1)}, f32[6,2,...) custom-call(bf16[48,4992]{1,0:T(8,128)(2,1)} %copy-done.8, ...), custom_call_target="tpu_custom_call" | custom-call | tf_op jit(solution)/shard_map/front/pallas_call | solution.py:840
  144.3 184.2 %back.1 = (bf16[1024,768]{1,0:T(8,128)(2,1)}, bf16[1024,768]{1,0:T(8,128)(2,1)}, bf16[1024,768]{1,0:T(8,128)(2,1)}, f32[48,4992]{1,0:T(8,128)}, bf16[48,384]{1,0:T(8,128)(2,1)}, /*index=5*/f32[8,128]{1,0:T(8,128)}) custom-call(bf16[1024,768]{1,0:T(8,128)(2,1)} %get-tuple-element.56.q_h, bf16[1024,768]{1,0:T(8,128)(2,1)} %get-tuple-element.57.k_h, ...), custom_call_target="tpu_custom_call" | custom-call | tf_op jit(solution)/shard_map/back/pallas_call | solution.py:1099
  328.6 1.0 select_convert_fusion.1
  329.6 1.2 slice.77
  331.6 0.6 add_multiply_fusion.5
  332.2 0.6 copy.84
  332.8 0.6 copy.86
  333.4 0.6 copy.88
  334.5 0.7 add_multiply_fusion.2
  335.3 0.6 add_multiply_fusion.4
  336.2 1.1 add_multiply_fusion.1
  337.3 1.0 add_multiply_fusion
  338.3 0.7 add_multiply_fusion.3
  339.6 0.7 copy.83
  340.3 0.7 copy.85
  341.0 0.7 copy.87
  341.9 0.7 compare_reduce_fusion
  342.9 1.6 pad_maximum_fusion.1
  344.5 0.5 copy-done
  345.0 0.6 copy-done.1
  346.3 1.6 pad_maximum_fusion
  (96 shorter events, 2.9 us)
Async XLA Ops:
  0.7 6.6 %copy-start.5 = (f32[4,384,48]{1,2,0:T(8,128)S(1)}, f32[4,384,48]{1,2,0:T(8,128)}, u32[]{:S(2)}) copy-start(f32[4,384,48]{1,2,0:T(8,128)} %param.38) | copy-start | bytes 884740
  1.4 6.0 %copy-start.33 = (s32[1,2]{1,0:T(1,128)S(1)}, s32[1,2]{1,0:T(1,128)}, u32[]{:S(2)}) copy-start(s32[1,2]{1,0:T(1,128)} %param.34) | copy-start | bytes 28
  7.4 2.3 copy-start.8
  144.1 187.4 %copy-start.24 = (f32[7,48]{1,0:T(8,128)S(1)}, f32[7,48]{1,0:T(8,128)}, u32[]{:S(2)}) copy-start(f32[7,48]{1,0:T(8,128)} %param.43) | copy-start | bytes 4036
  144.1 187.4 %copy-start.26 = (f32[7,48]{1,0:T(8,128)S(1)}, f32[7,48]{1,0:T(8,128)}, u32[]{:S(2)}) copy-start(f32[7,48]{1,0:T(8,128)} %param.61) | copy-start | bytes 4036
  144.2 187.4 %copy-start.27 = (f32[7,48]{1,0:T(8,128)S(1)}, f32[7,48]{1,0:T(8,128)}, u32[]{:S(2)}) copy-start(f32[7,48]{1,0:T(8,128)} %param.52) | copy-start | bytes 4036
  144.2 188.0 %copy-start.25 = (f32[6,1,24]{2,1,0:T(1,128)S(1)}, f32[6,1,24]{2,1,0:T(1,128)}, u32[]{:S(2)}) copy-start(f32[6,1,24]{2,1,0:T(1,128)} %param.42) | copy-start | bytes 1732
  144.2 188.0 %copy-start.28 = (f32[6,1,24]{2,1,0:T(1,128)S(1)}, f32[6,1,24]{2,1,0:T(1,128)}, u32[]{:S(2)}) copy-start(f32[6,1,24]{2,1,0:T(1,128)} %param.60) | copy-start | bytes 1732
  144.2 188.0 %copy-start.29 = (f32[6,1,24]{2,1,0:T(1,128)S(1)}, f32[6,1,24]{2,1,0:T(1,128)}, u32[]{:S(2)}) copy-start(f32[6,1,24]{2,1,0:T(1,128)} %param.51) | copy-start | bytes 1732
  144.2 189.8 %copy-start.30 = (f32[32]{0:T(128)S(1)}, f32[32]{0:T(128)}, u32[]{:S(2)}) copy-start(f32[32]{0:T(128)} %param.41) | copy-start | bytes 388
  144.2 189.7 %copy-start.31 = (f32[32]{0:T(128)S(1)}, f32[32]{0:T(128)}, u32[]{:S(2)}) copy-start(f32[32]{0:T(128)} %param.59) | copy-start | bytes 388
  144.2 189.7 %copy-start.32 = (f32[32]{0:T(128)S(1)}, f32[32]{0:T(128)}, u32[]{:S(2)}) copy-start(f32[32]{0:T(128)} %param.50) | copy-start | bytes 388
  144.2 190.3 %copy-start.16 = (f32[32,768]{1,0:T(8,128)S(1)}, f32[32,768]{1,0:T(8,128)}, u32[]{:S(2)}) copy-start(f32[32,768]{1,0:T(8,128)} %param.40) | copy-start | bytes 294916
  144.3 190.3 %copy-start.17 = (f32[32,768]{1,0:T(8,128)S(1)}, f32[32,768]{1,0:T(8,128)}, u32[]{:S(2)}) copy-start(f32[32,768]{1,0:T(8,128)} %param.58) | copy-start | bytes 294916
  144.3 190.3 %copy-start.18 = (f32[32,768]{1,0:T(8,128)S(1)}, f32[32,768]{1,0:T(8,128)}, u32[]{:S(2)}) copy-start(f32[32,768]{1,0:T(8,128)} %param.49) | copy-start | bytes 294916
  144.3 191.0 %copy-start.21 = (f32[8,512]{1,0:T(8,128)S(1)}, f32[8,512]{1,0:T(8,128)}, u32[]{:S(2)}) copy-start(f32[8,512]{1,0:T(8,128)} %param.39) | copy-start | bytes 49156
  144.3 191.0 %copy-start.22 = (f32[8,512]{1,0:T(8,128)S(1)}, f32[8,512]{1,0:T(8,128)}, u32[]{:S(2)}) copy-start(f32[8,512]{1,0:T(8,128)} %param.57) | copy-start | bytes 49156
  144.3 191.0 %copy-start.23 = (f32[8,512]{1,0:T(8,128)S(1)}, f32[8,512]{1,0:T(8,128)}, u32[]{:S(2)}) copy-start(f32[8,512]{1,0:T(8,128)} %param.48) | copy-start | bytes 49156
  328.5 7.4 %copy-start.6 = (f32[48,4992]{1,0:T(8,128)S(1)}, f32[48,4992]{1,0:T(8,128)}, u32[]{:S(2)}) copy-start(f32[48,4992]{1,0:T(8,128)} %get-tuple-element.78) | copy-start | bytes 2875396
  328.5 7.6 %copy-start.4 = (f32[48,4,384]{2,1,0:T(4,128)S(1)}, f32[48,4,384]{2,1,0:T(4,128)}, u32[]{:S(2)}) copy-start(f32[48,4,384]{2,1,0:T(4,128)} %param.37) | copy-start | bytes 884740
  328.6 7.6 %copy-start.10 = (f32[48,4,384]{2,1,0:T(4,128)S(1)}, f32[48,4,384]{2,1,0:T(4,128)}, u32[]{:S(2)}) copy-start(f32[48,4,384]{2,1,0:T(4,128)} %param.55) | copy-start | bytes 884740
  328.6 7.6 %copy-start.11 = (f32[48,4,384]{2,1,0:T(4,128)S(1)}, f32[48,4,384]{2,1,0:T(4,128)}, u32[]{:S(2)}) copy-start(f32[48,4,384]{2,1,0:T(4,128)} %param.46) | copy-start | bytes 884740
  336.1 2.2 copy-start.9
  336.2 2.1 copy-start.19
  336.2 2.1 copy-start.20
  337.3 1.8 copy-start.7
  337.3 1.8 copy-start.14
  337.3 1.8 copy-start.15
  339.2 2.5 copy-start.2
  339.2 2.5 copy-start.3
  342.9 2.1 copy-start
  342.9 2.7 copy-start.1
  (2 other events, 2.5 us)
